TPU v7x, 128 devices: a whole 4x4x4 slice. The times are simulated.
128 devices in a mesh: win: 4 (over z_lo, core), rcv: 32 (over x, y, z_hi).
Axes of the slice: x: 4, y: 4, z: 4 (z_hi: 2, z_lo: 2; z = z_hi * 2 + z_lo), core: 2. Of those that a mesh axis runs over, the one named last changes fastest.
Arguments:
- spectra: bfloat16 [32, 2, 1024, 4096], P('win', None, 'rcv'), may hold values from -6 to 6
- sources: bfloat16 [32, 2, 1024, 4096], P('win', None, 'rcv'), may hold values from -6 to 6
- usable: int32 [32, 1024], P('win', 'rcv'), may hold values 0 or 1
- owners: int32 [1], replicated, may hold values from 0 to 31
Outputs:
- correlations: float32 [32, 1024, 768], P('win', 'rcv')
All inputs are finite; a program needn't handle non-finite values. No bound on the sum of `usable` on one device may be relied on, other than what follows from the above.
Results may differ from a plain program's by a relative error of at most 0.013.
Values may be sent and summed in bfloat16 or wider, within the bound.
No kernel may reach another device: no remote copies, remote signals or barrier semaphores. Data moves between devices by JAX's collectives and lax.ppermute only.
A program may use at most 256 MiB of HBM per device.

v0:
```python
import math

import jax
import jax.numpy as jnp
from jax import lax
from jax.sharding import PartitionSpec as P

LAGS = 768


def from_root(value, axis, source):
    kept = jnp.where(lax.axis_index(axis) == source, value, 0).astype(value.dtype)
    return lax.psum(kept, axis)


def build_table(bins, lags, windows):
    frequency = jnp.arange(bins, dtype=jnp.int32)[:, None]
    lag_index = jnp.arange(lags, dtype=jnp.int32)[None, :] - lags // 2
    period = 2 * bins
    phases = jnp.mod(frequency * lag_index, period).astype(jnp.float32) * (2.0 * math.pi / period)
    weight = jnp.where(frequency == 0, 1.0, 2.0).astype(jnp.float32)
    scaling = 1.0 / math.sqrt(8.0 * bins * windows)
    return jnp.concatenate([weight * jnp.cos(phases), -weight * jnp.sin(phases)], 0) * scaling


def local(spectra, sources, usable, owners):
    flagged = usable.astype(jnp.bfloat16)[:, None, :, None]
    receivers = spectra * flagged
    own_sources = sources * flagged
    broadcast_block = from_root(own_sources, "rcv", owners[0])
    swapped = jnp.concatenate([receivers[:, 1:2], -receivers[:, 0:1]], 1)
    real_part = jnp.einsum(
        "wcsf,wcrf->srf", broadcast_block, receivers, preferred_element_type=jnp.float32
    )
    imag_part = jnp.einsum(
        "wcsf,wcrf->srf", broadcast_block, swapped, preferred_element_type=jnp.float32
    )
    partial_value = jnp.concatenate([real_part, imag_part], -1).astype(jnp.bfloat16)
    sources_all = partial_value.shape[0]
    channels = partial_value.shape[1]
    doubled = partial_value.shape[2]
    groups = lax.axis_size("win")
    local_sources = sources_all // groups
    table = build_table(doubled // 2, LAGS, spectra.shape[0] * groups)
    stacked = lax.psum_scatter(
        partial_value.astype(jnp.float32).astype(jnp.bfloat16),
        "win",
        scatter_dimension=0,
        tiled=True,
    ).astype(jnp.float32)
    lagged = jnp.dot(
        stacked.reshape(local_sources * channels, doubled),
        table,
        precision=lax.Precision.HIGHEST,
        preferred_element_type=jnp.float32,
    )
    return lagged.reshape(local_sources, channels, LAGS)


def solution(mesh):
    return jax.shard_map(
        local,
        mesh=mesh,
        in_specs=(P("win", None, "rcv", None), P("win", None, "rcv", None), P("win", "rcv"), P()),
        out_specs=P("win", "rcv", None),
        check_vma=False,
    )
```

profile of v0, /device:TPU:1, one launch (start us, length us, event | category | flops | bytes accessed | tf_op | source)
XLA Modules:
  0.0 719.3 jit_solution(10731206971965057161)
XLA Ops:
  6.5 0.0 all-reduce.2.cloned.1.call-start
  7.2 0.7 convert_element_type.14
  7.9 5.9 multiply_select_fusion
  13.7 0.0 all-reduce.2.cloned.1.call-update
  13.8 0.0 reduce-scatter.2.cloned.1.call-start
  13.8 18.2 %copy.5 = bf16[8,2,32,4096]{2,0,1,3:T(8,128)(2,1)} copy(bf16[8,2,32,4096]{3,2,1,0:T(8,128)(2,1)} %get-tuple-element.10) | data formatting | bytes 8388608 | tf_op jit(solution)/shard_map/mul | solution.py:28
  32.0 2.5 fusion.18
  34.5 2.3 pad_maximum_fusion.1
  36.8 18.2 %copy.8 = bf16[8,2,32,4096]{2,0,1,3:T(8,128)(2,1)} copy(bf16[8,2,32,4096]{3,2,1,0:T(8,128)(2,1)} %pad_maximum_fusion.1) | data formatting | bytes 8388608 | tf_op jit(solution)/shard_map/concatenate | solution.py:31
  55.0 307.1 %all-reduce.2.cloned.1.call-done = bf16[8,2,32,4096]{3,2,1,0:T(8,128)(2,1)} async-done(((bf16[8,2,32,4096]{3,2,1,0:T(8,128)(2,1)}), bf16[8,2,32,4096]{3,2,1,0:T(8,128)(2,1)}) %all-reduce.2.cloned.1.call-update) | async-done | bytes 4194320 | tf_op jit(solution)/shard_map/psum | solution.py:13
  362.1 18.1 %copy.6 = bf16[8,2,32,4096]{2,0,1,3:T(8,128)(2,1)} copy(bf16[8,2,32,4096]{3,2,1,0:T(8,128)(2,1)} %all-reduce.2.cloned.1.call-done) | data formatting | bytes 8388608 | tf_op jit(solution)/shard_map/psum | solution.py:13
  380.2 27.7 %fusion.20 = bf16[4096,32,32,1]{2,1,3,0:T(8,128)(2,1)} fusion(bf16[8,2,32,4096]{2,0,1,3:T(8,128)(2,1)} %copy.8, bf16[8,2,32,4096]{2,0,1,3:T(8,128)(2,1)} %copy.6), kind=kOutput, calls=%fused_computation.34 | convolution fusion | flops 134217728 | bytes 16777216 | tf_op jit(solution)/shard_map/wcsf,wcrf->srf/dot_general | solution.py:35
  407.9 38.0 %copy.9 = bf16[4096,32,32,1]{0,1,2,3:T(8,128)(2,1)} copy(bf16[4096,32,32,1]{2,1,3,0:T(8,128)(2,1)} %fusion.20) | data formatting | bytes 16777216 | tf_op jit(solution)/shard_map/wcsf,wcrf->srf/dot_general | solution.py:35
  445.9 27.7 %fusion.19 = bf16[4096,32,32,1]{2,1,3,0:T(8,128)(2,1)} fusion(bf16[8,2,32,4096]{2,0,1,3:T(8,128)(2,1)} %copy.5, bf16[8,2,32,4096]{2,0,1,3:T(8,128)(2,1)} %copy.6), kind=kOutput, calls=%fused_computation.33 | convolution fusion | flops 134217728 | bytes 16777216 | tf_op jit(solution)/shard_map/wcsf,wcrf->srf/dot_general | solution.py:32
  473.6 38.0 %copy.7 = bf16[4096,32,32,1]{0,1,2,3:T(8,128)(2,1)} copy(bf16[4096,32,32,1]{2,1,3,0:T(8,128)(2,1)} %fusion.19) | data formatting | bytes 16777216 | tf_op jit(solution)/shard_map/wcsf,wcrf->srf/dot_general | solution.py:32
  511.6 6.9 fusion.12
  518.5 6.7 pad_maximum_fusion
  525.2 0.0 reduce-scatter.2.cloned.1.call-update
  525.3 52.2 %cosine_multiply_fusion = (f32[4096,768]{1,0:T(8,128)}, f32[4096,768]{1,0:T(8,128)}) fusion(s32[768]{0:T(1024)S(1)} %iota_add_fusion, f32[4096]{0:T(1024)S(1)} %get-tuple-element.13, f32[4096]{0:T(1024)S(1)} %get-tuple-element.14), kind=kLoop, calls=%fused_computation.16 | loop fusion | flops 50331648 | bytes 25201664 | tf_op jit(solution)/shard_map/mul | solution.py:23
  577.4 116.3 %reduce-scatter.2.cloned.1.call-done = bf16[8,32,8192]{2,1,0:T(8,128)(2,1)} async-done(((bf16[32,32,8192]{2,1,0:T(8,128)(2,1)}), bf16[8,32,8192]{2,1,0:T(8,128)(2,1)}) %reduce-scatter.2.cloned.1.call-update) | async-done | bytes 4194320 | tf_op jit(solution)/shard_map/reduce_scatter | solution.py:45
  693.8 18.7 %fusion.1 = f32[8,32,768]{2,1,0:T(8,128)} fusion(bf16[8,32,8192]{2,1,0:T(8,128)(2,1)} %reduce-scatter.2.cloned.1.call-done, f32[4096,768]{1,0:T(8,128)} %get-tuple-element.8, f32[4096,768]{1,0:T(8,128)} %get-tuple-element.7), kind=kOutput, calls=%fused_computation.2 | convolution fusion | flops 19339935744 | bytes 30146560 | tf_op jit(solution)/shard_map/dot_general | solution.py:51
  (2 shorter events, 0.0 us)
Async XLA Ops:
  6.5 355.5 %all-reduce.2.cloned.1.call-start = ((), (), s32[]{:S(2)}) async-start(), calls=%async_computation.1 | async-start | bytes 8388608 | tf_op jit(solution)/shard_map/psum | solution.py:13
  13.8 680.0 %reduce-scatter.2.cloned.1.call-start = ((), (), s32[]{:S(2)}) async-start(), calls=%async_computation.2 | async-start | bytes 20971520 | tf_op jit(solution)/shard_map/reduce_scatter | solution.py:45
Sparse Core Ops, SparseCore 0:
  13.9 348.1 all-reduce.1
  525.4 168.3 reduce-scatter.1
where the time goes:
time: 723 us; the launch traced here: 719 us
  waiting for transfers between devices  423 us (59%)
  local copies, waits for them, and re-layouts  137 us (19%)
  matrix products  74.1 us (10%)
  other arithmetic  70.3 us (10%)
  between operations  14.1 us (2%)
    psum x1, waiting for transfers between devices, from_root(): return lax.psum(kept, axis)  307 us
    reduce_scatter x1, waiting for transfers between devices, local(): lax.psum_scatter(partial_value.astype(jnp.float32).astype(jnp.bfloat16),...  116 us
    mul x1, other arithmetic, build_table(): weight * jnp.cos(phases)  52.2 us
    dot_general x1, local copies, waits for them, and re-layouts, local(): jnp.einsum('wcsf,wcrf->srf', broadcast_block, swapped, preferred_element_...  38 us
    dot_general x1, local copies, waits for them, and re-layouts, local(): jnp.einsum('wcsf,wcrf->srf', broadcast_block, receivers, preferred_elemen...  38 us
    dot_general x1, matrix products, local(): jnp.einsum('wcsf,wcrf->srf', broadcast_block, swapped, preferred_element_...  27.7 us
    dot_general x1, matrix products, local(): jnp.einsum('wcsf,wcrf->srf', broadcast_block, receivers, preferred_elemen...  27.7 us
    dot_general x1, matrix products, local(): jnp.dot(stacked.reshape(local_sources * channels, doubled), table, precis...  18.7 us
  transfers between devices with their start and end apart: 2, of which 2 were waited for; matrix products, arithmetic and copies ran while one was open for 13% of the time, Pallas kernels for 0%

commit v1 on v0

v1 whole, which is shorter than its diff:
```python
import math

import jax
import jax.numpy as jnp
from jax import lax
from jax.experimental import pallas as pl
from jax.experimental.pallas import tpu as pltpu
from jax.sharding import PartitionSpec as P

LAGS = 768
LANES = 128
QUARTERS = 4
WIDE = 256
LIMIT = 8
ROWS = 8
MIB = 2**20


def build_table(bins, lags, windows):
    fine = 64
    low = jnp.arange(fine, dtype=jnp.int32)[:, None]
    high = jnp.arange(bins // fine, dtype=jnp.int32)[:, None] * fine
    lag = jnp.arange(lags, dtype=jnp.int32)[None, :] - lags // 2
    period = 2 * bins
    unit = 2.0 * math.pi / period
    angle_low = jnp.mod(low * lag, period).astype(jnp.float32) * unit
    angle_high = jnp.mod(high * lag, period).astype(jnp.float32) * unit
    scaling = 2.0 / math.sqrt(8.0 * bins * windows)
    tables = (jnp.cos(angle_low) * scaling, jnp.sin(angle_low) * scaling, jnp.cos(angle_high), jnp.sin(angle_high))

    def kernel(cos_low, sin_low, cos_high, sin_high, o_ref):
        def one(h, carry):
            cos_h, sin_h = cos_high[pl.ds(h, 1)], sin_high[pl.ds(h, 1)]
            start = pl.multiple_of(h * fine, fine)
            real = cos_h * cos_low[...] - sin_h * sin_low[...]
            imag = sin_h * cos_low[...] + cos_h * sin_low[...]
            row = lax.broadcasted_iota(jnp.int32, real.shape, 0)
            real = jnp.where(jnp.logical_and(h == 0, row == 0), 0.5 * real, real)
            o_ref[pl.ds(start, fine)] = real.astype(jnp.bfloat16)
            o_ref[pl.ds(bins + start, fine)] = (-imag).astype(jnp.bfloat16)
            return carry

        lax.fori_loop(0, bins // fine, one, 0)

    in_vmem = pl.BlockSpec(memory_space=pltpu.VMEM)
    return pl.pallas_call(
        kernel,
        in_specs=[in_vmem] * 4,
        out_specs=in_vmem,
        out_shape=jax.ShapeDtypeStruct((2 * bins, lags), jnp.bfloat16),
        compiler_params=pltpu.CompilerParams(vmem_limit_bytes=8 * MIB),
        cost_estimate=pl.CostEstimate(flops=16 * bins * lags, bytes_accessed=4 * bins * lags, transcendentals=0),
    )(*tables)


def cut_sources(sources, flags, place):
    windows, parts, channels, bins = sources.shape
    columns = bins // LANES
    wide = columns // QUARTERS
    total = windows * parts * columns

    def kernel(place_ref, s_hbm, f_ref, *refs):
        outs = refs[:QUARTERS]
        held, rows, sems = refs[QUARTERS:]

        @pl.when(place_ref[0] == 1)
        def _():
            def fetch(w):
                return pltpu.make_async_copy(s_hbm.at[w], held.at[w], sems.at[w])

            for w in range(windows):
                fetch(w).start()

            def one(w, carry):
                fetch(w).wait()
                for c in range(parts):
                    for column in range(columns):
                        lanes = slice(column * LANES, (column + 1) * LANES)
                        rows[column] = held[w, c, :, lanes].astype(jnp.float32) * f_ref[w]
                    for d in range(QUARTERS):
                        m = lax.rem(place_ref[1] + d, QUARTERS)
                        for column in range(columns):
                            spot = ((column // wide) * windows * parts + w * parts + c) * wide + column % wide
                            outs[d][spot] = rows[column, pl.ds(m, ROWS, stride=QUARTERS)].astype(jnp.bfloat16)
                return carry

            lax.fori_loop(0, windows, one, 0)

    in_vmem = pl.BlockSpec(memory_space=pltpu.VMEM)
    return pl.pallas_call(
        kernel,
        in_specs=[pl.BlockSpec(memory_space=pltpu.SMEM), pl.BlockSpec(memory_space=pl.ANY), in_vmem],
        out_specs=[in_vmem] * QUARTERS,
        scratch_shapes=[
            pltpu.VMEM(sources.shape, jnp.bfloat16),
            pltpu.VMEM((columns, channels, LANES), jnp.float32),
            pltpu.SemaphoreType.DMA((windows,)),
        ],
        out_shape=[jax.ShapeDtypeStruct((total, ROWS, LANES), jnp.bfloat16)] * QUARTERS,
        compiler_params=pltpu.CompilerParams(vmem_limit_bytes=16 * MIB),
        cost_estimate=pl.CostEstimate(flops=2 * sources.size, bytes_accessed=4 * sources.size, transcendentals=0),
    )(place, sources, flags)


def mask_receivers(spectra, flags):
    windows, parts, receivers, bins = spectra.shape
    columns = bins // LANES

    def kernel(r_ref, f_ref, o_ref):
        def one(column, carry):
            lanes = pl.ds(pl.multiple_of(column * LANES, LANES), LANES)
            for w in range(windows):
                real = r_ref[w, 0, :, lanes].astype(jnp.float32) * f_ref[w]
                imag = r_ref[w, 1, :, lanes].astype(jnp.float32) * f_ref[w]
                o_ref[column, w, 0] = real
                o_ref[column, w, 1] = imag
                o_ref[column, w, 2] = real + imag
            return carry

        lax.fori_loop(0, columns, one, 0)

    in_vmem = pl.BlockSpec(memory_space=pltpu.VMEM)
    return pl.pallas_call(
        kernel,
        in_specs=[in_vmem] * 2,
        out_specs=in_vmem,
        out_shape=jax.ShapeDtypeStruct((columns, windows, 3, receivers, LANES), jnp.float32),
        compiler_params=pltpu.CompilerParams(vmem_limit_bytes=8 * MIB),
        cost_estimate=pl.CostEstimate(flops=4 * spectra.size, bytes_accessed=8 * spectra.size, transcendentals=0),
    )(spectra, flags)


def lag_quarter(receiving, tiles, table, place):
    columns, windows, _, receivers, _ = receiving.shape
    parts = 2
    bins = columns * LANES
    total = tiles.shape[0]
    doubled, lags = table.shape
    wide = columns // QUARTERS
    half = ROWS * receivers // 2

    def kernel(place_ref, r_ref, s_ref, t_ref, kept_ref, given_ref, sf, cross, lagged):
        def one(column, carry):
            near = lax.rem(place_ref[0] + QUARTERS - column // wide, QUARTERS)
            base = near * (total // QUARTERS) + lax.rem(column, wide)
            to_real = pl.ds(pl.multiple_of(column * LANES, LANES), LANES)
            to_imag = pl.ds(pl.multiple_of(bins + column * LANES, LANES), LANES)
            for w in range(windows):
                real = s_ref[base + w * parts * wide].astype(jnp.float32)
                imag = s_ref[base + (w * parts + 1) * wide].astype(jnp.float32)
                sf[w, 0] = real
                sf[w, 1] = imag
                sf[w, 2] = real - imag
            for s0 in range(0, ROWS, 4):
                for r0 in range(0, receivers, 16):
                    sums = [[None] * 3 for _ in range(4)]
                    for w in range(windows):
                        right = [r_ref[column, w, j, r0 : r0 + 16] for j in range(3)]
                        for s in range(4):
                            for j in range(3):
                                left = jnp.broadcast_to(sf[w, j, s0 + s : s0 + s + 1], (16, LANES))
                                term = left * right[j]
                                sums[s][j] = term if sums[s][j] is None else sums[s][j] + term
                    for s in range(4):
                        first, second, third = sums[s]
                        row = (s0 + s) * receivers + r0
                        cross[row : row + 16, to_real] = (first + second).astype(jnp.bfloat16)
                        cross[row : row + 16, to_imag] = (third - first + second).astype(jnp.bfloat16)
            return carry

        lax.fori_loop(0, columns, one, 0)
        for n in range(0, lags, WIDE):
            part = slice(n, n + WIDE)
            lagged[:, part] = jnp.dot(cross[...], t_ref[:, part], preferred_element_type=jnp.float32)
        chip = place_ref[1]
        kept_ref[...] = lagged[pl.ds(pl.multiple_of(chip * half, half), half)]
        given_ref[...] = lagged[pl.ds(pl.multiple_of((1 - chip) * half, half), half)].astype(jnp.bfloat16)

    in_vmem = pl.BlockSpec(memory_space=pltpu.VMEM)
    return pl.pallas_call(
        kernel,
        in_specs=[pl.BlockSpec(memory_space=pltpu.SMEM), in_vmem, in_vmem, in_vmem],
        out_specs=[in_vmem] * 2,
        scratch_shapes=[
            pltpu.VMEM((windows, 3, ROWS, LANES), jnp.float32),
            pltpu.VMEM((2 * half, doubled), jnp.bfloat16),
            pltpu.VMEM((2 * half, lags), jnp.float32),
        ],
        out_shape=[
            jax.ShapeDtypeStruct((half, lags), jnp.float32),
            jax.ShapeDtypeStruct((half, lags), jnp.bfloat16),
        ],
        compiler_params=pltpu.CompilerParams(vmem_limit_bytes=LIMIT * MIB),
        cost_estimate=pl.CostEstimate(
            flops=2 * ROWS * receivers * doubled * lags * 3, bytes_accessed=2 * table.size, transcendentals=0
        ),
    )(place, receiving, tiles, table)


def split_cores(kept, received, place):
    rows, lags = kept[0].shape
    half = rows // 2

    def kernel(place_ref, *refs):
        kept_refs, received_refs = refs[:QUARTERS], refs[QUARTERS : 2 * QUARTERS]
        mine_ref, given_ref = refs[2 * QUARTERS :]
        core = place_ref[1]
        mine = pl.ds(pl.multiple_of(core * half, half), half)
        other = pl.ds(pl.multiple_of((1 - core) * half, half), half)
        for d in range(QUARTERS):
            m = lax.rem(place_ref[0] + QUARTERS - d, QUARTERS)
            mine_ref[m] = kept_refs[d][mine] + received_refs[d][mine].astype(jnp.float32)
            total = kept_refs[d][other] + received_refs[d][other].astype(jnp.float32)
            given_ref[m] = total.astype(jnp.bfloat16)

    in_vmem = pl.BlockSpec(memory_space=pltpu.VMEM)
    return pl.pallas_call(
        kernel,
        in_specs=[pl.BlockSpec(memory_space=pltpu.SMEM)] + [in_vmem] * (2 * QUARTERS),
        out_specs=[in_vmem] * 2,
        out_shape=[
            jax.ShapeDtypeStruct((QUARTERS, half, lags), jnp.float32),
            jax.ShapeDtypeStruct((QUARTERS, half, lags), jnp.bfloat16),
        ],
        compiler_params=pltpu.CompilerParams(vmem_limit_bytes=8 * MIB),
        cost_estimate=pl.CostEstimate(flops=8 * rows * lags, bytes_accessed=32 * rows * lags, transcendentals=0),
    )(place, *kept, *received)


class Grid:
    def __init__(self):
        self.pairs = {}
        side = 4
        for axis in range(2):
            for step in range(1, side):
                moves = []
                for win in range(4):
                    for x in range(side):
                        for y in range(side):
                            for z in range(2):
                                on_x = axis == win % 2
                                nx, ny = ((x + step) % side, y) if on_x else (x, (y + step) % side)
                                moves.append((win * 32 + (x * side + y) * 2 + z, win * 32 + (nx * side + ny) * 2 + z))
                self.pairs[axis, step] = moves

    def move(self, value, axis, step):
        return lax.ppermute(value, ("win", "rcv"), self.pairs[axis, step])

    def flip(self, value):
        return lax.ppermute(value, "rcv", [(i, i ^ 1) for i in range(32)])

    @staticmethod
    def place(index, core):
        x, y = index // 8, (index // 2) % 4
        return jnp.where(core == 0, x, y), jnp.where(core == 0, y, x), index % 2


def pick(values, chosen):
    result = values[0]
    for value, this in zip(values[1:], chosen):
        result = jnp.where(this, value, result)
    return result


def at(value, index):
    return lax.dynamic_index_in_dim(value, index, 0, keepdims=False)


def local(spectra, sources, usable, owners):
    windows, parts, channels, bins = spectra.shape
    grid = Grid()
    steps = range(1, QUARTERS)
    owner = owners[0].astype(jnp.int32)
    win = lax.axis_index("win")
    chip, core = win // 2, win % 2
    rcv = lax.axis_index("rcv")
    u, v, z = grid.place(rcv, core)
    owner_u, owner_v, owner_z = grid.place(owner, core)
    cut_place = jnp.stack([(rcv == owner).astype(jnp.int32), v])
    lag_place = jnp.stack([u, chip])
    end_place = jnp.stack([v, core])
    to_bins = [((u + d) % QUARTERS).astype(jnp.uint32) for d in range(QUARTERS)]
    off_v = [(v - owner_v) % QUARTERS == d for d in steps]
    off_u = [(u - owner_u) % QUARTERS == d for d in steps]
    same_z = z == owner_z
    scalars = (cut_place, lag_place, end_place, to_bins, off_v, off_u, same_z)
    scalars, usable = lax.optimization_barrier((scalars, usable))
    cut_place, lag_place, end_place, to_bins, off_v, off_u, same_z = scalars

    flags = jnp.broadcast_to(usable.astype(jnp.float32)[:, :, None], (windows, channels, LANES))
    table = build_table(bins, LAGS, windows * lax.axis_size("win"))
    receiving = mask_receivers(spectra, flags)
    tiles = windows * parts * (bins // LANES)
    cut = cut_sources(sources, flags, cut_place)
    cut = [part.reshape(QUARTERS, tiles // QUARTERS, ROWS, LANES) for part in cut]
    dealt = [cut[0]] + [grid.move(cut[d], 1, d) for d in steps]
    mine = pick(dealt, off_v)
    mine, table, receiving = lax.optimization_barrier((mine, table, receiving))
    dealt = [at(mine, to_bins[0])] + [grid.move(at(mine, to_bins[d]), 0, d) for d in steps]
    mine = pick(dealt, off_u)
    mine = jnp.where(same_z, mine, grid.flip(mine))
    row = jnp.stack([mine] + [grid.move(mine, 0, d) for d in steps])
    quarters = [row] + [grid.move(row, 1, d) for d in steps]

    kept, received = [None] * QUARTERS, [None] * QUARTERS
    for d in (0, 1, 3, 2):
        kept[d], given = lag_quarter(receiving, quarters[d].reshape(tiles, ROWS, LANES), table, lag_place)
        received[d] = lax.ppermute(given, "win", [(0, 2), (2, 0), (1, 3), (3, 1)])
    kept, given = split_cores(kept, received, end_place)
    result = kept + lax.ppermute(given, "win", [(0, 1), (1, 0), (2, 3), (3, 2)]).astype(jnp.float32)
    return result.reshape(QUARTERS, 2, channels, LAGS).transpose(1, 0, 2, 3).reshape(2 * QUARTERS, channels, LAGS)


def solution(mesh):
    return jax.shard_map(
        local,
        mesh=mesh,
        in_specs=(P("win", None, "rcv", None), P("win", None, "rcv", None), P("win", "rcv"), P()),
        out_specs=P("win", "rcv", None),
        check_vma=False,
    )
```

time: 723 us -> 137 us (0.19)
  waiting for transfers between devices: 423 us -> 41.7 us
  local copies, waits for them, and re-layouts: 137 us -> 5.46 us
  matrix products: 74.1 us -> 0 us
  other arithmetic: 70.3 us -> 2.97 us
  Pallas kernels: 0 us -> 55.7 us
  starting transfers between devices: 0.04 us -> 29.6 us
  between operations: 14.1 us -> 1.03 us
    psum x1 -> x0, waiting for transfers between devices: 307 us -> none  [from_root(): return lax.psum(kept, axis)]
    reduce_scatter x1 -> x0, waiting for transfers between devices: 116 us -> none  [local(): lax.psum_scatter(partial_value.astype(jnp.float32).astype(jnp.bfloat16),...]
    dot_general x2 -> x0, local copies, waits for them, and re-layouts: 76.1 us -> none  [the longest x1 38 us: local(): jnp.einsum('wcsf,wcrf->srf', broadcast_block, swapped, preferred_element_...]
    dot_general x3 -> x0, matrix products: 74.1 us -> none  [the longest x1 27.7 us: local(): jnp.einsum('wcsf,wcrf->srf', broadcast_block, swapped, preferred_element_...]
    pallas_call x0 -> x8, Pallas kernels: none -> 55.7 us  [the longest x4 48.7 us: lag_quarter(): pl.pallas_call(kernel, in_specs=[pl.BlockSpec(memory_space=pltpu.SMEM), i...]
    mul x1, other arithmetic: 52.2 us -> 0.01 us  [build_table(): high = jnp.arange(bins // fine, dtype=jnp.int32)[:, None] * fine]
    ppermute x0 -> x18, waiting for transfers between devices: none -> 41.7 us  [the longest x12 33.3 us: move(): return lax.ppermute(value, ('win', 'rcv'), self.pairs[axis, step])]
    ppermute x0 -> x18, starting transfers between devices: none -> 29.6 us  [the longest x12 12.3 us: move(): return lax.ppermute(value, ('win', 'rcv'), self.pairs[axis, step])]
  transfers between devices with their start and end apart: 2 -> 18, of which waited for: 2 -> 11; matrix products, arithmetic and copies ran while one was open for 13% -> 1% of each run, Pallas kernels for 0% -> 40%
where the time goes in v1:
time: 137 us; the launch traced here: 136 us
  Pallas kernels  55.7 us (41%)
  waiting for transfers between devices  41.7 us (30%)
  starting transfers between devices  29.6 us (22%)
  local copies, waits for them, and re-layouts  5.46 us (4%)
  other arithmetic  2.97 us (2%)
    pallas_call x4, Pallas kernels, lag_quarter(): pl.pallas_call(kernel, in_specs=[pl.BlockSpec(memory_space=pltpu.SMEM), i...  48.7 us
    ppermute x12, waiting for transfers between devices, move(): return lax.ppermute(value, ('win', 'rcv'), self.pairs[axis, step])  33.3 us
    ppermute x12, starting transfers between devices, move(): return lax.ppermute(value, ('win', 'rcv'), self.pairs[axis, step])  12.3 us
    ppermute x1, starting transfers between devices, local(): lax.ppermute(given, 'win', [(0, 1), (1, 0), (2, 3), (3, 2)])  9.35 us
    unnamed x4, local copies, waits for them, and re-layouts  4.37 us
    ppermute x4, starting transfers between devices, local(): received[d] = lax.ppermute(given, 'win', [(0, 2), (2, 0), (1, 3), (3, 1)])  4.26 us
    pallas_call x1, Pallas kernels, build_table(): pl.pallas_call(kernel, in_specs=[in_vmem] * 4, out_specs=in_vmem, out_sha...  4.21 us
    ppermute x1, waiting for transfers between devices, flip(): return lax.ppermute(value, 'rcv', [(i, i ^ 1) for i in range(32)])  3.76 us
  transfers between devices with their start and end apart: 18, of which 11 were waited for; matrix products, arithmetic and copies ran while one was open for 1% of the time, Pallas kernels for 40%

profile of v1, /device:TPU:1, one launch (start us, length us, event | category | flops | bytes accessed | tf_op | source)
XLA Modules:
  0.0 136.4 jit_solution(3783458855953504013)
XLA Ops:
  0.9 0.1 pad_add_fusion.1.place_ref
  1.0 0.1 pad_add_fusion
  1.0 0.7 convert_element_type.33
  1.7 0.1 broadcast_in_dim.2.f_ref
  1.8 2.2 %copy-done = bf16[8,2,32,4096]{3,2,1,0:T(8,128)(2,1)S(1)} copy-done((bf16[8,2,32,4096]{3,2,1,0:T(8,128)(2,1)S(1)}, bf16[8,2,32,4096]{3,2,1,0:T(8,128)(2,1)}, u32[]{:S(2)}) %copy-start) | copy-done | bytes 4194328
  4.0 0.6 shard_map.46
  4.6 3.4 %collective-permute-start = (bf16[4,128,8,128]{3,2,1,0:T(8,128)(2,1)S(1)}, bf16[4,128,8,128]{3,2,1,0:T(8,128)(2,1)S(1)}, u32[]{:S(2)}, u32[]{:S(2)}) collective-permute-start(bf16[4,128,8,128]{3,2,1,0:T(8,128)(2,1)S(1)} %bitcast.44), channel_id=1, source_target_pairs={{0,6},{1,7},{2,0},{3,1},{4,2},{5,3},{6,4},{7,5},{8,14},{9,15},{10,... | collective-permute-start | bytes 3145736 | tf_op jit(solution)/shard_map/ppermute | solution.py:247
  8.0 0.5 collective-permute-start.1
  8.5 0.6 collective-permute-start.2
  9.1 2.2 %copy-done.1 = bf16[8,2,32,4096]{3,2,1,0:T(8,128)(2,1)S(1)} copy-done((bf16[8,2,32,4096]{3,2,1,0:T(8,128)(2,1)S(1)}, bf16[8,2,32,4096]{3,2,1,0:T(8,128)(2,1)}, u32[]{:S(2)}) %copy-start.1) | copy-done | bytes 4194328
  11.3 1.4 %shard_map.48.r_ref = f32[32,8,3,32,128]{4,3,2,1,0:T(8,128)S(1)} custom-call(bf16[8,2,32,4096]{3,2,1,0:T(8,128)(2,1)S(1)} %copy-done.1, f32[8,32,128]{2,1,0:T(8,128)S(1)} %broadcast_in_dim.2.f_ref), custom_call_target="tpu_custom_call" | custom-call | flops 8388608 | bytes 16777216 | tf_op jit(solution)/shard_map/pallas_call | solution.py:123
  12.8 1.6 %fusion.11 = (f32[64,768]{1,0:T(8,128)S(1)}, f32[64,768]{1,0:T(8,128)S(1)}, f32[64,768]{1,0:T(8,128)S(1)}, f32[64,768]{1,0:T(8,128)S(1)}) fusion(s32[768]{0:T(1024)S(1)} %iota_add_fusion, s32[64]{0:T(128)S(1)} %iota_multiply_fusion), kind=kLoop, calls=%fused_computation.29 | loop fusion | flops 1474560 | bytes 789760 | tf_op jit(solution)/shard_map/sin | solution.py:29
  14.4 4.2 %shard_map.47.t_ref = bf16[8192,768]{1,0:T(8,128)(2,1)S(1)} custom-call(f32[64,768]{1,0:T(8,128)S(1)} %get-tuple-element.75.cos_low, f32[64,768]{1,0:T(8,128)S(1)} %get-tuple-element.74.sin_low, f32[64,768]{1,0:T(8,128)S(1)} %get-tuple-element.73.cos_high, f32[64,768]{1,0:T(8,128)S(1)} %get-tuple-element.72.sin_high), custom_call_target="tpu_custom_call" | custom-call | flops 50331648 | bytes 12582912 | tf_op jit(solution)/shard_map/pallas_call | solution.py:46
  18.6 12.4 %collective-permute-done = bf16[4,128,8,128]{3,2,1,0:T(8,128)(2,1)S(1)} collective-permute-done((bf16[4,128,8,128]{3,2,1,0:T(8,128)(2,1)S(1)}, bf16[4,128,8,128]{3,2,1,0:T(8,128)(2,1)S(1)}, u32[]{:S(2)}, u32[]{:S(2)}) %collective-permute-start) | collective-permute-done | bytes 1048608 | tf_op jit(solution)/shard_map/ppermute | solution.py:247
  31.0 3.7 %collective-permute-done.2 = bf16[4,128,8,128]{3,2,1,0:T(8,128)(2,1)S(1)} collective-permute-done((bf16[4,128,8,128]{3,2,1,0:T(8,128)(2,1)S(1)}, bf16[4,128,8,128]{3,2,1,0:T(8,128)(2,1)S(1)}, u32[]{:S(2)}, u32[]{:S(2)}) %collective-permute-start.2) | collective-permute-done | bytes 1048608 | tf_op jit(solution)/shard_map/ppermute | solution.py:247
  34.7 0.3 select_select_fusion
  35.0 2.5 %collective-permute-start.3 = (bf16[128,8,128]{2,1,0:T(8,128)(2,1)S(1)}, bf16[128,8,128]{2,1,0:T(8,128)(2,1)S(1)}, u32[]{:S(2)}, u32[]{:S(2)}) collective-permute-start(bf16[128,8,128]{2,1,0:T(8,128)(2,1)S(1)} %get-tuple-element.71), channel_id=1, source_target_pairs={{0,24},{1,25},{2,26},{3,27},{4,28},{5,29},{6,30},{7,31},{8,0},{9,1... | collective-permute-start | bytes 786440 | tf_op jit(solution)/shard_map/ppermute | solution.py:247
  37.6 0.3 collective-permute-start.4
  37.9 0.7 collective-permute-start.5
  38.6 5.1 %collective-permute-done.3 = bf16[128,8,128]{2,1,0:T(8,128)(2,1)S(1)} collective-permute-done((bf16[128,8,128]{2,1,0:T(8,128)(2,1)S(1)}, bf16[128,8,128]{2,1,0:T(8,128)(2,1)S(1)}, u32[]{:S(2)}, u32[]{:S(2)}) %collective-permute-start.3) | collective-permute-done | bytes 262176 | tf_op jit(solution)/shard_map/ppermute | solution.py:247
  43.7 0.9 collective-permute-done.4
  44.6 2.8 %collective-permute-done.5 = bf16[128,8,128]{2,1,0:T(8,128)(2,1)S(1)} collective-permute-done((bf16[128,8,128]{2,1,0:T(8,128)(2,1)S(1)}, bf16[128,8,128]{2,1,0:T(8,128)(2,1)S(1)}, u32[]{:S(2)}, u32[]{:S(2)}) %collective-permute-start.5) | collective-permute-done | bytes 262176 | tf_op jit(solution)/shard_map/ppermute | solution.py:247
  47.4 3.7 %collective-permute-start.6 = (bf16[128,8,128]{2,1,0:T(8,128)(2,1)S(1)}, bf16[128,8,128]{2,1,0:T(8,128)(2,1)S(1)}, u32[]{:S(2)}, u32[]{:S(2)}) collective-permute-start(bf16[128,8,128]{2,1,0:T(8,128)(2,1)S(1)} %fusion.1), channel_id=1, source_target_pairs={{0,1},{1,0},{2,3},{3,2},{4,5},{5,4},{6,7},{7,6},{8,9},{9,8},{10,11... | collective-permute-start | bytes 786440 | tf_op jit(solution)/shard_map/ppermute | solution.py:250
  51.1 3.8 %collective-permute-done.6 = bf16[128,8,128]{2,1,0:T(8,128)(2,1)S(1)} collective-permute-done((bf16[128,8,128]{2,1,0:T(8,128)(2,1)S(1)}, bf16[128,8,128]{2,1,0:T(8,128)(2,1)S(1)}, u32[]{:S(2)}, u32[]{:S(2)}) %collective-permute-start.6) | collective-permute-done | bytes 262176 | tf_op jit(solution)/shard_map/ppermute | solution.py:250
  54.9 0.1 collective-permute-start.7
  55.0 1.5 %collective-permute-start.8 = (bf16[128,8,128]{2,1,0:T(8,128)(2,1)S(1)}, bf16[128,8,128]{2,1,0:T(8,128)(2,1)S(1)}, u32[]{:S(2)}, u32[]{:S(2)}) collective-permute-start(bf16[128,8,128]{2,1,0:T(8,128)(2,1)S(1)} %broadcast_select_fusion), channel_id=1, source_target_pairs={{0,16},{1,17},{2,18},{3,19},{4,20},{5,21},{6,22},{7,23},{8,24},{9,... | collective-permute-start | bytes 786440 | tf_op jit(solution)/shard_map/ppermute | solution.py:247
  56.5 1.2 collective-permute-start.9
  57.7 6.9 %collective-permute-done.7 = bf16[128,8,128]{2,1,0:T(8,128)(2,1)S(1)} collective-permute-done((bf16[128,8,128]{2,1,0:T(8,128)(2,1)S(1)}, bf16[128,8,128]{2,1,0:T(8,128)(2,1)S(1)}, u32[]{:S(2)}, u32[]{:S(2)}) %collective-permute-start.7) | collective-permute-done | bytes 262176 | tf_op jit(solution)/shard_map/ppermute | solution.py:247
  64.5 0.6 collective-permute-done.9
  65.1 0.1 pad_maximum_fusion
  65.3 0.4 collective-permute-start.12
  65.7 0.7 collective-permute-start.11
  66.3 0.5 collective-permute-start.10
  66.8 12.2 %shard_map.49 = (f32[128,768]{1,0:T(8,128)S(1)}, bf16[128,768]{1,0:T(8,128)(2,1)S(1)}) custom-call(s32[2]{0:T(128)S(1)} %pad_add_fusion.1.place_ref, f32[32,8,3,32,128]{4,3,2,1,0:T(8,128)S(1)} %shard_map.48.r_ref, bf16[512,8,128]{2,1,0:T(8,128)(2,1)S(1)} %bitcast.39, bf16[8192,768]{1,0:T(8,128)(2,1)S(1)} %shard_map.47.t_ref), custom_call_target="tpu_custom_call" | custom-call | flops 9663676416 | bytes 12582912 | tf_op jit(solution)/shard_map/pallas_call | solution.py:180
  79.0 1.3 collective-permute-start.13
  80.3 1.0 collective-permute-done.12
  81.2 12.2 %shard_map.52 = (f32[128,768]{1,0:T(8,128)S(1)}, bf16[128,768]{1,0:T(8,128)(2,1)S(1)}) custom-call(s32[2]{0:T(128)S(1)} %pad_add_fusion.1.place_ref, f32[32,8,3,32,128]{4,3,2,1,0:T(8,128)S(1)} %shard_map.48.r_ref, bf16[512,8,128]{2,1,0:T(8,128)(2,1)S(1)} %bitcast.46, bf16[8192,768]{1,0:T(8,128)(2,1)S(1)} %shard_map.47.t_ref), custom_call_target="tpu_custom_call" | custom-call | flops 9663676416 | bytes 12582912 | tf_op jit(solution)/shard_map/pallas_call | solution.py:180
  93.4 1.4 %collective-permute-start.16 = (bf16[128,768]{1,0:T(8,128)(2,1)S(1)}, bf16[128,768]{1,0:T(8,128)(2,1)S(1)}, u32[]{:S(2)}, u32[]{:S(2)}) collective-permute-start(bf16[128,768]{1,0:T(8,128)(2,1)S(1)} %get-tuple-element.66), channel_id=1, source_target_pairs={{0,64},{64,0},{32,96},{96,32},{1,65},{65,1},{33,97},{97,33},{2,66}... | collective-permute-start | bytes 589832 | tf_op jit(solution)/shard_map/ppermute | solution.py:308
  94.8 12.2 %shard_map.51 = (f32[128,768]{1,0:T(8,128)S(1)}, bf16[128,768]{1,0:T(8,128)(2,1)S(1)}) custom-call(s32[2]{0:T(128)S(1)} %pad_add_fusion.1.place_ref, f32[32,8,3,32,128]{4,3,2,1,0:T(8,128)S(1)} %shard_map.48.r_ref, bf16[512,8,128]{2,1,0:T(8,128)(2,1)S(1)} %bitcast.45, bf16[8192,768]{1,0:T(8,128)(2,1)S(1)} %shard_map.47.t_ref), custom_call_target="tpu_custom_call" | custom-call | flops 9663676416 | bytes 12582912 | tf_op jit(solution)/shard_map/pallas_call | solution.py:180
  107.0 0.3 collective-permute-start.15
  107.2 12.2 %shard_map.50 = (f32[128,768]{1,0:T(8,128)S(1)}, bf16[128,768]{1,0:T(8,128)(2,1)S(1)}) custom-call(s32[2]{0:T(128)S(1)} %pad_add_fusion.1.place_ref, f32[32,8,3,32,128]{4,3,2,1,0:T(8,128)S(1)} %shard_map.48.r_ref, bf16[512,8,128]{2,1,0:T(8,128)(2,1)S(1)} %bitcast.42, bf16[8192,768]{1,0:T(8,128)(2,1)S(1)} %shard_map.47.t_ref), custom_call_target="tpu_custom_call" | custom-call | flops 9663676416 | bytes 12582912 | tf_op jit(solution)/shard_map/pallas_call | solution.py:180
  119.4 1.4 %collective-permute-start.14 = (bf16[128,768]{1,0:T(8,128)(2,1)S(1)}, bf16[128,768]{1,0:T(8,128)(2,1)S(1)}, u32[]{:S(2)}, u32[]{:S(2)}) collective-permute-start(bf16[128,768]{1,0:T(8,128)(2,1)S(1)} %get-tuple-element.64), channel_id=1, source_target_pairs={{0,64},{64,0},{32,96},{96,32},{1,65},{65,1},{33,97},{97,33},{2,66}... | collective-permute-start | bytes 589832 | tf_op jit(solution)/shard_map/ppermute | solution.py:308
  120.8 3.2 %collective-permute-done.14.refs_5_ = bf16[128,768]{1,0:T(8,128)(2,1)S(1)} collective-permute-done((bf16[128,768]{1,0:T(8,128)(2,1)S(1)}, bf16[128,768]{1,0:T(8,128)(2,1)S(1)}, u32[]{:S(2)}, u32[]{:S(2)}) %collective-permute-start.14) | collective-permute-done | bytes 196640 | tf_op jit(solution)/shard_map/ppermute | solution.py:308
  124.0 0.7 shard_map.53
  124.7 9.3 %collective-permute-start.17 = (bf16[4,64,768]{2,1,0:T(8,128)(2,1)S(1)}, bf16[4,64,768]{2,1,0:T(8,128)(2,1)S(1)}, u32[]{:S(2)}, u32[]{:S(2)}) collective-permute-start(bf16[4,64,768]{2,1,0:T(8,128)(2,1)S(1)} %get-tuple-element.68), channel_id=1, source_target_pairs={{0,32},{32,0},{64,96},{96,64},{1,33},{33,1},{65,97},{97,65},{2,34}... | collective-permute-start | bytes 1179656 | tf_op jit(solution)/shard_map/ppermute | solution.py:310
  134.1 1.3 collective-permute-done.17
  135.4 0.1 convert_add_fusion
  135.5 0.9 copy.5
  (14 shorter events, 0.2 us)
Async XLA Ops:
  1.8 2.2 %copy-start = (bf16[8,2,32,4096]{3,2,1,0:T(8,128)(2,1)S(1)}, bf16[8,2,32,4096]{3,2,1,0:T(8,128)(2,1)}, u32[]{:S(2)}) copy-start(bf16[8,2,32,4096]{3,2,1,0:T(8,128)(2,1)} %s_hbm.1) | copy-start | bytes 12582916
  4.6 26.4 %collective-permute-start = (bf16[4,128,8,128]{3,2,1,0:T(8,128)(2,1)S(1)}, bf16[4,128,8,128]{3,2,1,0:T(8,128)(2,1)S(1)}, u32[]{:S(2)}, u32[]{:S(2)}) collective-permute-start(bf16[4,128,8,128]{3,2,1,0:T(8,128)(2,1)S(1)} %bitcast.44), channel_id=1, source_target_pairs={{0,6},{1,7},{2,0},{3,1},{4,2},{5,3},{6,4},{7,5},{8,14},{9,15},{10,... | collective-permute-start | bytes 3145736 | tf_op jit(solution)/shard_map/ppermute | solution.py:247
  8.0 23.0 %collective-permute-start.1 = (bf16[4,128,8,128]{3,2,1,0:T(8,128)(2,1)S(1)}, bf16[4,128,8,128]{3,2,1,0:T(8,128)(2,1)S(1)}, u32[]{:S(2)}, u32[]{:S(2)}) collective-permute-start(bf16[4,128,8,128]{3,2,1,0:T(8,128)(2,1)S(1)} %bitcast.43), channel_id=1, source_target_pairs={{0,4},{1,5},{2,6},{3,7},{4,0},{5,1},{6,2},{7,3},{8,12},{9,13},{10,... | collective-permute-start | bytes 3145736 | tf_op jit(solution)/shard_map/ppermute | solution.py:247
  8.5 26.2 %collective-permute-start.2 = (bf16[4,128,8,128]{3,2,1,0:T(8,128)(2,1)S(1)}, bf16[4,128,8,128]{3,2,1,0:T(8,128)(2,1)S(1)}, u32[]{:S(2)}, u32[]{:S(2)}) collective-permute-start(bf16[4,128,8,128]{3,2,1,0:T(8,128)(2,1)S(1)} %bitcast.41), channel_id=1, source_target_pairs={{0,2},{1,3},{2,4},{3,5},{4,6},{5,7},{6,0},{7,1},{8,10},{9,11},{10,... | collective-permute-start | bytes 3145736 | tf_op jit(solution)/shard_map/ppermute | solution.py:247
  9.1 2.2 %copy-start.1 = (bf16[8,2,32,4096]{3,2,1,0:T(8,128)(2,1)S(1)}, bf16[8,2,32,4096]{3,2,1,0:T(8,128)(2,1)}, u32[]{:S(2)}) copy-start(bf16[8,2,32,4096]{3,2,1,0:T(8,128)(2,1)} %r_ref.1) | copy-start | bytes 12582916
  35.0 8.6 %collective-permute-start.3 = (bf16[128,8,128]{2,1,0:T(8,128)(2,1)S(1)}, bf16[128,8,128]{2,1,0:T(8,128)(2,1)S(1)}, u32[]{:S(2)}, u32[]{:S(2)}) collective-permute-start(bf16[128,8,128]{2,1,0:T(8,128)(2,1)S(1)} %get-tuple-element.71), channel_id=1, source_target_pairs={{0,24},{1,25},{2,26},{3,27},{4,28},{5,29},{6,30},{7,31},{8,0},{9,1... | collective-permute-start | bytes 786440 | tf_op jit(solution)/shard_map/ppermute | solution.py:247
  37.6 7.1 %collective-permute-start.4 = (bf16[128,8,128]{2,1,0:T(8,128)(2,1)S(1)}, bf16[128,8,128]{2,1,0:T(8,128)(2,1)S(1)}, u32[]{:S(2)}, u32[]{:S(2)}) collective-permute-start(bf16[128,8,128]{2,1,0:T(8,128)(2,1)S(1)} %get-tuple-element.70), channel_id=1, source_target_pairs={{0,16},{1,17},{2,18},{3,19},{4,20},{5,21},{6,22},{7,23},{8,24},{9,... | collective-permute-start | bytes 786440 | tf_op jit(solution)/shard_map/ppermute | solution.py:247
  37.9 9.5 %collective-permute-start.5 = (bf16[128,8,128]{2,1,0:T(8,128)(2,1)S(1)}, bf16[128,8,128]{2,1,0:T(8,128)(2,1)S(1)}, u32[]{:S(2)}, u32[]{:S(2)}) collective-permute-start(bf16[128,8,128]{2,1,0:T(8,128)(2,1)S(1)} %get-tuple-element.69), channel_id=1, source_target_pairs={{0,8},{1,9},{2,10},{3,11},{4,12},{5,13},{6,14},{7,15},{8,16},{9,17... | collective-permute-start | bytes 786440 | tf_op jit(solution)/shard_map/ppermute | solution.py:247
  47.4 7.4 %collective-permute-start.6 = (bf16[128,8,128]{2,1,0:T(8,128)(2,1)S(1)}, bf16[128,8,128]{2,1,0:T(8,128)(2,1)S(1)}, u32[]{:S(2)}, u32[]{:S(2)}) collective-permute-start(bf16[128,8,128]{2,1,0:T(8,128)(2,1)S(1)} %fusion.1), channel_id=1, source_target_pairs={{0,1},{1,0},{2,3},{3,2},{4,5},{5,4},{6,7},{7,6},{8,9},{9,8},{10,11... | collective-permute-start | bytes 786440 | tf_op jit(solution)/shard_map/ppermute | solution.py:250
  54.9 9.6 %collective-permute-start.7 = (bf16[128,8,128]{2,1,0:T(8,128)(2,1)S(1)}, bf16[128,8,128]{2,1,0:T(8,128)(2,1)S(1)}, u32[]{:S(2)}, u32[]{:S(2)}) collective-permute-start(bf16[128,8,128]{2,1,0:T(8,128)(2,1)S(1)} %broadcast_select_fusion), channel_id=1, source_target_pairs={{0,8},{1,9},{2,10},{3,11},{4,12},{5,13},{6,14},{7,15},{8,16},{9,17... | collective-permute-start | bytes 786440 | tf_op jit(solution)/shard_map/ppermute | solution.py:247
  55.0 9.5 %collective-permute-start.8 = (bf16[128,8,128]{2,1,0:T(8,128)(2,1)S(1)}, bf16[128,8,128]{2,1,0:T(8,128)(2,1)S(1)}, u32[]{:S(2)}, u32[]{:S(2)}) collective-permute-start(bf16[128,8,128]{2,1,0:T(8,128)(2,1)S(1)} %broadcast_select_fusion), channel_id=1, source_target_pairs={{0,16},{1,17},{2,18},{3,19},{4,20},{5,21},{6,22},{7,23},{8,24},{9,... | collective-permute-start | bytes 786440 | tf_op jit(solution)/shard_map/ppermute | solution.py:247
  56.5 8.6 %collective-permute-start.9 = (bf16[128,8,128]{2,1,0:T(8,128)(2,1)S(1)}, bf16[128,8,128]{2,1,0:T(8,128)(2,1)S(1)}, u32[]{:S(2)}, u32[]{:S(2)}) collective-permute-start(bf16[128,8,128]{2,1,0:T(8,128)(2,1)S(1)} %broadcast_select_fusion), channel_id=1, source_target_pairs={{0,24},{1,25},{2,26},{3,27},{4,28},{5,29},{6,30},{7,31},{8,0},{9,1... | collective-permute-start | bytes 786440 | tf_op jit(solution)/shard_map/ppermute | solution.py:247
  65.3 15.9 %collective-permute-start.12 = (bf16[4,128,8,128]{3,2,1,0:T(8,128)(2,1)S(1)}, bf16[4,128,8,128]{3,2,1,0:T(8,128)(2,1)S(1)}, u32[]{:S(2)}, u32[]{:S(2)}) collective-permute-start(bf16[4,128,8,128]{3,2,1,0:T(8,128)(2,1)S(1)} %pad_maximum_fusion), channel_id=1, source_target_pairs={{0,6},{1,7},{2,0},{3,1},{4,2},{5,3},{6,4},{7,5},{8,14},{9,15},{10,... | collective-permute-start | bytes 3145736 | tf_op jit(solution)/shard_map/ppermute | solution.py:247
  65.7 29.1 %collective-permute-start.11 = (bf16[4,128,8,128]{3,2,1,0:T(8,128)(2,1)S(1)}, bf16[4,128,8,128]{3,2,1,0:T(8,128)(2,1)S(1)}, u32[]{:S(2)}, u32[]{:S(2)}) collective-permute-start(bf16[4,128,8,128]{3,2,1,0:T(8,128)(2,1)S(1)} %pad_maximum_fusion), channel_id=1, source_target_pairs={{0,4},{1,5},{2,6},{3,7},{4,0},{5,1},{6,2},{7,3},{8,12},{9,13},{10,... | collective-permute-start | bytes 3145736 | tf_op jit(solution)/shard_map/ppermute | solution.py:247
  66.3 40.9 %collective-permute-start.10 = (bf16[4,128,8,128]{3,2,1,0:T(8,128)(2,1)S(1)}, bf16[4,128,8,128]{3,2,1,0:T(8,128)(2,1)S(1)}, u32[]{:S(2)}, u32[]{:S(2)}) collective-permute-start(bf16[4,128,8,128]{3,2,1,0:T(8,128)(2,1)S(1)} %pad_maximum_fusion), channel_id=1, source_target_pairs={{0,2},{1,3},{2,4},{3,5},{4,6},{5,7},{6,0},{7,1},{8,10},{9,11},{10,... | collective-permute-start | bytes 3145736 | tf_op jit(solution)/shard_map/ppermute | solution.py:247
  79.0 41.8 %collective-permute-start.13 = (bf16[128,768]{1,0:T(8,128)(2,1)S(1)}, bf16[128,768]{1,0:T(8,128)(2,1)S(1)}, u32[]{:S(2)}, u32[]{:S(2)}) collective-permute-start(bf16[128,768]{1,0:T(8,128)(2,1)S(1)} %get-tuple-element.63), channel_id=1, source_target_pairs={{0,64},{64,0},{32,96},{96,32},{1,65},{65,1},{33,97},{97,33},{2,66}... | collective-permute-start | bytes 589832 | tf_op jit(solution)/shard_map/ppermute | solution.py:308
  93.4 27.4 %collective-permute-start.16 = (bf16[128,768]{1,0:T(8,128)(2,1)S(1)}, bf16[128,768]{1,0:T(8,128)(2,1)S(1)}, u32[]{:S(2)}, u32[]{:S(2)}) collective-permute-start(bf16[128,768]{1,0:T(8,128)(2,1)S(1)} %get-tuple-element.66), channel_id=1, source_target_pairs={{0,64},{64,0},{32,96},{96,32},{1,65},{65,1},{33,97},{97,33},{2,66}... | collective-permute-start | bytes 589832 | tf_op jit(solution)/shard_map/ppermute | solution.py:308
  107.0 13.8 %collective-permute-start.15 = (bf16[128,768]{1,0:T(8,128)(2,1)S(1)}, bf16[128,768]{1,0:T(8,128)(2,1)S(1)}, u32[]{:S(2)}, u32[]{:S(2)}) collective-permute-start(bf16[128,768]{1,0:T(8,128)(2,1)S(1)} %get-tuple-element.65), channel_id=1, source_target_pairs={{0,64},{64,0},{32,96},{96,32},{1,65},{65,1},{33,97},{97,33},{2,66}... | collective-permute-start | bytes 589832 | tf_op jit(solution)/shard_map/ppermute | solution.py:308
  119.4 4.6 %collective-permute-start.14 = (bf16[128,768]{1,0:T(8,128)(2,1)S(1)}, bf16[128,768]{1,0:T(8,128)(2,1)S(1)}, u32[]{:S(2)}, u32[]{:S(2)}) collective-permute-start(bf16[128,768]{1,0:T(8,128)(2,1)S(1)} %get-tuple-element.64), channel_id=1, source_target_pairs={{0,64},{64,0},{32,96},{96,32},{1,65},{65,1},{33,97},{97,33},{2,66}... | collective-permute-start | bytes 589832 | tf_op jit(solution)/shard_map/ppermute | solution.py:308
  124.7 10.7 %collective-permute-start.17 = (bf16[4,64,768]{2,1,0:T(8,128)(2,1)S(1)}, bf16[4,64,768]{2,1,0:T(8,128)(2,1)S(1)}, u32[]{:S(2)}, u32[]{:S(2)}) collective-permute-start(bf16[4,64,768]{2,1,0:T(8,128)(2,1)S(1)} %get-tuple-element.68), channel_id=1, source_target_pairs={{0,32},{32,0},{64,96},{96,64},{1,33},{33,1},{65,97},{97,65},{2,34}... | collective-permute-start | bytes 1179656 | tf_op jit(solution)/shard_map/ppermute | solution.py:310

commit v2 on v1

--- a/solution.py
+++ b/solution.py
@@ -11,7 +11,8 @@
 LANES = 128
 QUARTERS = 4
 WIDE = 256
-LIMIT = 8
+LIMIT = 16
+GROUPS = ((0,), (1, 3), (2,))
 ROWS = 8
 MIB = 2**20
 
@@ -130,93 +131,108 @@
     )(spectra, flags)
 
 
-def lag_quarter(receiving, tiles, table, place):
+def lag_quarters(receiving, tiles, table, place, side=None):
     columns, windows, _, receivers, _ = receiving.shape
     parts = 2
     bins = columns * LANES
-    total = tiles.shape[0]
+    total = tiles[0].shape[0]
+    number = len(tiles)
     doubled, lags = table.shape
     wide = columns // QUARTERS
     half = ROWS * receivers // 2
 
-    def kernel(place_ref, r_ref, s_ref, t_ref, kept_ref, given_ref, sf, cross, lagged):
+    sides = (0, 1) if side is None else (side,)
+    shapes = [
+        jax.ShapeDtypeStruct((number * half, lags), jnp.float32),
+        jax.ShapeDtypeStruct((number * half, lags), jnp.bfloat16),
+    ]
+
+    def kernel(place_ref, r_ref, t_ref, *refs):
+        outs = refs[number : number + len(sides)]
+        sf, cross = refs[number + len(sides) :]
+        chip = place_ref[1]
+
         def one(column, carry):
             near = lax.rem(place_ref[0] + QUARTERS - column // wide, QUARTERS)
             base = near * (total // QUARTERS) + lax.rem(column, wide)
             to_real = pl.ds(pl.multiple_of(column * LANES, LANES), LANES)
             to_imag = pl.ds(pl.multiple_of(bins + column * LANES, LANES), LANES)
-            for w in range(windows):
-                real = s_ref[base + w * parts * wide].astype(jnp.float32)
-                imag = s_ref[base + (w * parts + 1) * wide].astype(jnp.float32)
-                sf[w, 0] = real
-                sf[w, 1] = imag
-                sf[w, 2] = real - imag
-            for s0 in range(0, ROWS, 4):
-                for r0 in range(0, receivers, 16):
-                    sums = [[None] * 3 for _ in range(4)]
-                    for w in range(windows):
-                        right = [r_ref[column, w, j, r0 : r0 + 16] for j in range(3)]
+            for q in range(number):
+                for w in range(windows):
+                    real = refs[q][base + w * parts * wide].astype(jnp.float32)
+                    imag = refs[q][base + (w * parts + 1) * wide].astype(jnp.float32)
+                    if side is not None:
+                        first = chip == side
+                        real = jnp.where(first, real[:4], real[4:])
+                        imag = jnp.where(first, imag[:4], imag[4:])
+                    sf[q, w, 0] = real
+                    sf[q, w, 1] = imag
+                    sf[q, w, 2] = real - imag
+                for s0 in range(0, 4 * len(sides), 4):
+                    for r0 in range(0, receivers, 16):
+                        sums = [[None] * 3 for _ in range(4)]
+                        for w in range(windows):
+                            right = [r_ref[column, w, j, r0 : r0 + 16] for j in range(3)]
+                            for s in range(4):
+                                for j in range(3):
+                                    left = jnp.broadcast_to(sf[q, w, j, s0 + s : s0 + s + 1], (16, LANES))
+                                    term = left * right[j]
+                                    sums[s][j] = term if sums[s][j] is None else sums[s][j] + term
                         for s in range(4):
-                            for j in range(3):
-                                left = jnp.broadcast_to(sf[w, j, s0 + s : s0 + s + 1], (16, LANES))
-                                term = left * right[j]
-                                sums[s][j] = term if sums[s][j] is None else sums[s][j] + term
-                    for s in range(4):
-                        first, second, third = sums[s]
-                        row = (s0 + s) * receivers + r0
-                        cross[row : row + 16, to_real] = (first + second).astype(jnp.bfloat16)
-                        cross[row : row + 16, to_imag] = (third - first + second).astype(jnp.bfloat16)
+                            first, second, third = sums[s]
+                            turn = lax.rem(chip + s0 // 4, 2) * number * half + q * half if side is None else q * half
+                            row = pl.ds(pl.multiple_of(turn + s * receivers + r0, 16), 16)
+                            cross[row, to_real] = (first + second).astype(jnp.bfloat16)
+                            cross[row, to_imag] = (third - first + second).astype(jnp.bfloat16)
             return carry
 
         lax.fori_loop(0, columns, one, 0)
         for n in range(0, lags, WIDE):
             part = slice(n, n + WIDE)
-            lagged[:, part] = jnp.dot(cross[...], t_ref[:, part], preferred_element_type=jnp.float32)
-        chip = place_ref[1]
-        kept_ref[...] = lagged[pl.ds(pl.multiple_of(chip * half, half), half)]
-        given_ref[...] = lagged[pl.ds(pl.multiple_of((1 - chip) * half, half), half)].astype(jnp.bfloat16)
-
-    in_vmem = pl.BlockSpec(memory_space=pltpu.VMEM)
-    return pl.pallas_call(
-        kernel,
-        in_specs=[pl.BlockSpec(memory_space=pltpu.SMEM), in_vmem, in_vmem, in_vmem],
-        out_specs=[in_vmem] * 2,
+            value = jnp.dot(cross[...], t_ref[:, part], preferred_element_type=jnp.float32)
+            for i, out in enumerate(outs):
+                out[:, part] = value[i * number * half : (i + 1) * number * half].astype(out.dtype)
+
+    in_vmem = pl.BlockSpec(memory_space=pltpu.VMEM)
+    return pl.pallas_call(
+        kernel,
+        in_specs=[pl.BlockSpec(memory_space=pltpu.SMEM)] + [in_vmem] * (2 + number),
+        out_specs=[in_vmem] * len(sides),
         scratch_shapes=[
-            pltpu.VMEM((windows, 3, ROWS, LANES), jnp.float32),
-            pltpu.VMEM((2 * half, doubled), jnp.bfloat16),
-            pltpu.VMEM((2 * half, lags), jnp.float32),
+            pltpu.VMEM((number, windows, 3, 4 * len(sides), LANES), jnp.float32),
+            pltpu.VMEM((len(sides) * number * half, doubled), jnp.bfloat16),
         ],
-        out_shape=[
-            jax.ShapeDtypeStruct((half, lags), jnp.float32),
-            jax.ShapeDtypeStruct((half, lags), jnp.bfloat16),
-        ],
+        out_shape=[shapes[i] for i in sides],
         compiler_params=pltpu.CompilerParams(vmem_limit_bytes=LIMIT * MIB),
         cost_estimate=pl.CostEstimate(
-            flops=2 * ROWS * receivers * doubled * lags * 3, bytes_accessed=2 * table.size, transcendentals=0
+            flops=len(sides) * number * half * 2 * doubled * lags * 3, bytes_accessed=2 * table.size, transcendentals=0
         ),
-    )(place, receiving, tiles, table)
-
-
-def split_cores(kept, received, place):
+    )(place, receiving, table, *tiles)
+
+
+def split_cores(kept, received, groups, place):
     rows, lags = kept[0].shape
+    rows = rows // len(groups[0])
     half = rows // 2
+    count = len(groups)
 
     def kernel(place_ref, *refs):
-        kept_refs, received_refs = refs[:QUARTERS], refs[QUARTERS : 2 * QUARTERS]
-        mine_ref, given_ref = refs[2 * QUARTERS :]
+        kept_refs, received_refs = refs[:count], refs[count : 2 * count]
+        mine_ref, given_ref = refs[2 * count :]
         core = place_ref[1]
-        mine = pl.ds(pl.multiple_of(core * half, half), half)
-        other = pl.ds(pl.multiple_of((1 - core) * half, half), half)
-        for d in range(QUARTERS):
-            m = lax.rem(place_ref[0] + QUARTERS - d, QUARTERS)
-            mine_ref[m] = kept_refs[d][mine] + received_refs[d][mine].astype(jnp.float32)
-            total = kept_refs[d][other] + received_refs[d][other].astype(jnp.float32)
-            given_ref[m] = total.astype(jnp.bfloat16)
-
-    in_vmem = pl.BlockSpec(memory_space=pltpu.VMEM)
-    return pl.pallas_call(
-        kernel,
-        in_specs=[pl.BlockSpec(memory_space=pltpu.SMEM)] + [in_vmem] * (2 * QUARTERS),
+        for group, kept_ref, received_ref in zip(groups, kept_refs, received_refs):
+            for i, d in enumerate(group):
+                mine = pl.ds(pl.multiple_of(i * rows + core * half, half), half)
+                other = pl.ds(pl.multiple_of(i * rows + (1 - core) * half, half), half)
+                m = lax.rem(place_ref[0] + QUARTERS - d, QUARTERS)
+                mine_ref[m] = kept_ref[mine] + received_ref[mine].astype(jnp.float32)
+                total = kept_ref[other] + received_ref[other].astype(jnp.float32)
+                given_ref[m] = total.astype(jnp.bfloat16)
+
+    in_vmem = pl.BlockSpec(memory_space=pltpu.VMEM)
+    return pl.pallas_call(
+        kernel,
+        in_specs=[pl.BlockSpec(memory_space=pltpu.SMEM)] + [in_vmem] * (2 * count),
         out_specs=[in_vmem] * 2,
         out_shape=[
             jax.ShapeDtypeStruct((QUARTERS, half, lags), jnp.float32),
@@ -300,13 +316,24 @@
     mine = pick(dealt, off_u)
     mine = jnp.where(same_z, mine, grid.flip(mine))
     row = jnp.stack([mine] + [grid.move(mine, 0, d) for d in steps])
-    quarters = [row] + [grid.move(row, 1, d) for d in steps]
-
-    kept, received = [None] * QUARTERS, [None] * QUARTERS
-    for d in (0, 1, 3, 2):
-        kept[d], given = lag_quarter(receiving, quarters[d].reshape(tiles, ROWS, LANES), table, lag_place)
-        received[d] = lax.ppermute(given, "win", [(0, 2), (2, 0), (1, 3), (3, 1)])
-    kept, given = split_cores(kept, received, end_place)
+    quarters = [row, grid.move(row, 1, 1), None, grid.move(row, 1, 3)]
+
+    kept, received = [], []
+    for group in GROUPS:
+        if group == GROUPS[1]:
+            row, quarters[1], quarters[3] = lax.optimization_barrier((row, quarters[1], quarters[3]))
+            quarters[2] = grid.move(row, 1, 2)
+        blocks = [quarters[d].reshape(tiles, ROWS, LANES) for d in group]
+        if group != GROUPS[-1]:
+            mine, given = lag_quarters(receiving, blocks, table, lag_place)
+        else:
+            (given,) = lag_quarters(receiving, blocks, table, lag_place, 1)
+            given, lag_place = lax.optimization_barrier((given, lag_place))
+            (mine,) = lag_quarters(receiving, blocks, table, lag_place, 0)
+        mine, lag_place = lax.optimization_barrier((mine, lag_place))
+        kept.append(mine)
+        received.append(lax.ppermute(given, "win", [(0, 2), (2, 0), (1, 3), (3, 1)]))
+    kept, given = split_cores(kept, received, GROUPS, end_place)
     result = kept + lax.ppermute(given, "win", [(0, 1), (1, 0), (2, 3), (3, 2)]).astype(jnp.float32)
     return result.reshape(QUARTERS, 2, channels, LAGS).transpose(1, 0, 2, 3).reshape(2 * QUARTERS, channels, LAGS)
 

time: 137 us -> 130 us (0.949)
  waiting for transfers between devices: 41.7 us -> 34.9 us
    ppermute x12, waiting for transfers between devices: 33.3 us -> 29.3 us  [move(): return lax.ppermute(value, ('win', 'rcv'), self.pairs[axis, step])]
    ppermute x4 -> x3, waiting for transfers between devices: 3.22 us -> 0.01 us  [local(): lax.ppermute(given, 'win', [(0, 2), (2, 0), (1, 3), (3, 1)])]
    ppermute x12, starting transfers between devices: 12.3 us -> 15.4 us  [move(): return lax.ppermute(value, ('win', 'rcv'), self.pairs[axis, step])]
    ppermute x1, starting transfers between devices: 9.35 us -> 6.62 us  [local(): lax.ppermute(given, 'win', [(0, 1), (1, 0), (2, 3), (3, 2)])]
    ppermute x4 -> x3, starting transfers between devices: 4.26 us -> 2.71 us  [local(): lax.ppermute(given, 'win', [(0, 2), (2, 0), (1, 3), (3, 1)])]
  transfers between devices with their start and end apart: 18 -> 17, of which waited for: 11 -> 10; matrix products, arithmetic and copies ran while one was open for 1% -> 1% of each run, Pallas kernels for 40% -> 43%
where the time goes in v2:
time: 130 us; the launch traced here: 129 us
  Pallas kernels  56.3 us (43%)
  waiting for transfers between devices  34.9 us (27%)
  starting transfers between devices  28.4 us (22%)
  local copies, waits for them, and re-layouts  5.46 us (4%)
  other arithmetic  2.98 us (2%)
    pallas_call x4, Pallas kernels, lag_quarters(): pl.pallas_call(kernel, in_specs=[pl.BlockSpec(memory_space=pltpu.SMEM)] +...  49.3 us
    ppermute x12, waiting for transfers between devices, move(): return lax.ppermute(value, ('win', 'rcv'), self.pairs[axis, step])  29.3 us
    ppermute x12, starting transfers between devices, move(): return lax.ppermute(value, ('win', 'rcv'), self.pairs[axis, step])  15.4 us
    ppermute x1, starting transfers between devices, local(): lax.ppermute(given, 'win', [(0, 1), (1, 0), (2, 3), (3, 2)])  6.62 us
    unnamed x4, local copies, waits for them, and re-layouts  4.37 us
    ppermute x1, waiting for transfers between devices, flip(): return lax.ppermute(value, 'rcv', [(i, i ^ 1) for i in range(32)])  4.23 us
    pallas_call x1, Pallas kernels, build_table(): pl.pallas_call(kernel, in_specs=[in_vmem] * 4, out_specs=in_vmem, out_sha...  4.21 us
    ppermute x1, starting transfers between devices, flip(): return lax.ppermute(value, 'rcv', [(i, i ^ 1) for i in range(32)])  3.68 us
  transfers between devices with their start and end apart: 17, of which 10 were waited for; matrix products, arithmetic and copies ran while one was open for 1% of the time, Pallas kernels for 43%

profile of v2, /device:TPU:1, one launch (start us, length us, event | category | flops | bytes accessed | tf_op | source)
XLA Modules:
  0.0 129.0 jit_solution(13858548708462161813)
XLA Ops:
  0.8 0.1 pad_add_fusion.1.place_ref
  0.9 0.1 pad_add_fusion
  1.0 0.7 convert_element_type.33
  1.7 0.1 broadcast_in_dim.2.f_ref
  1.7 0.0 copy-start
  1.8 2.2 %copy-done = bf16[8,2,32,4096]{3,2,1,0:T(8,128)(2,1)S(1)} copy-done((bf16[8,2,32,4096]{3,2,1,0:T(8,128)(2,1)S(1)}, bf16[8,2,32,4096]{3,2,1,0:T(8,128)(2,1)}, u32[]{:S(2)}) %copy-start) | copy-done | bytes 4194328
  3.9 0.6 shard_map.46
  4.6 3.7 %collective-permute-start.1 = (bf16[4,128,8,128]{3,2,1,0:T(8,128)(2,1)S(1)}, bf16[4,128,8,128]{3,2,1,0:T(8,128)(2,1)S(1)}, u32[]{:S(2)}, u32[]{:S(2)}) collective-permute-start(bf16[4,128,8,128]{3,2,1,0:T(8,128)(2,1)S(1)} %bitcast.45), channel_id=1, source_target_pairs={{0,4},{1,5},{2,6},{3,7},{4,0},{5,1},{6,2},{7,3},{8,12},{9,13},{10,... | collective-permute-start | bytes 3145736 | tf_op jit(solution)/shard_map/ppermute | solution.py:263
  8.2 0.9 collective-permute-start
  9.1 0.6 collective-permute-start.2
  9.7 2.2 %copy-done.1 = bf16[8,2,32,4096]{3,2,1,0:T(8,128)(2,1)S(1)} copy-done((bf16[8,2,32,4096]{3,2,1,0:T(8,128)(2,1)S(1)}, bf16[8,2,32,4096]{3,2,1,0:T(8,128)(2,1)}, u32[]{:S(2)}) %copy-start.1) | copy-done | bytes 4194328
  11.9 1.4 %shard_map.48.r_ref = f32[32,8,3,32,128]{4,3,2,1,0:T(8,128)S(1)} custom-call(bf16[8,2,32,4096]{3,2,1,0:T(8,128)(2,1)S(1)} %copy-done.1, f32[8,32,128]{2,1,0:T(8,128)S(1)} %broadcast_in_dim.2.f_ref), custom_call_target="tpu_custom_call" | custom-call | flops 8388608 | bytes 16777216 | tf_op jit(solution)/shard_map/pallas_call | solution.py:124
  13.3 1.6 %fusion.11 = (f32[64,768]{1,0:T(8,128)S(1)}, f32[64,768]{1,0:T(8,128)S(1)}, f32[64,768]{1,0:T(8,128)S(1)}, f32[64,768]{1,0:T(8,128)S(1)}) fusion(s32[768]{0:T(1024)S(1)} %iota_add_fusion, s32[64]{0:T(128)S(1)} %iota_multiply_fusion), kind=kLoop, calls=%fused_computation.29 | loop fusion | flops 1474560 | bytes 789760 | tf_op jit(solution)/shard_map/sin | solution.py:30
  14.9 4.2 %shard_map.47.t_ref = bf16[8192,768]{1,0:T(8,128)(2,1)S(1)} custom-call(f32[64,768]{1,0:T(8,128)S(1)} %get-tuple-element.87.cos_low, f32[64,768]{1,0:T(8,128)S(1)} %get-tuple-element.86.sin_low, f32[64,768]{1,0:T(8,128)S(1)} %get-tuple-element.85.cos_high, f32[64,768]{1,0:T(8,128)S(1)} %get-tuple-element.84.sin_high), custom_call_target="tpu_custom_call" | custom-call | flops 50331648 | bytes 12582912 | tf_op jit(solution)/shard_map/pallas_call | solution.py:47
  19.1 1.6 %collective-permute-done.1 = bf16[4,128,8,128]{3,2,1,0:T(8,128)(2,1)S(1)} collective-permute-done((bf16[4,128,8,128]{3,2,1,0:T(8,128)(2,1)S(1)}, bf16[4,128,8,128]{3,2,1,0:T(8,128)(2,1)S(1)}, u32[]{:S(2)}, u32[]{:S(2)}) %collective-permute-start.1) | collective-permute-done | bytes 1048608 | tf_op jit(solution)/shard_map/ppermute | solution.py:263
  20.8 11.5 %collective-permute-done = bf16[4,128,8,128]{3,2,1,0:T(8,128)(2,1)S(1)} collective-permute-done((bf16[4,128,8,128]{3,2,1,0:T(8,128)(2,1)S(1)}, bf16[4,128,8,128]{3,2,1,0:T(8,128)(2,1)S(1)}, u32[]{:S(2)}, u32[]{:S(2)}) %collective-permute-start) | collective-permute-done | bytes 1048608 | tf_op jit(solution)/shard_map/ppermute | solution.py:263
  32.3 0.2 select_select_fusion
  32.5 0.1 dynamic-slice_bitcast_fusion
  32.6 1.6 %collective-permute-start.5 = (bf16[128,8,128]{2,1,0:T(8,128)(2,1)S(1)}, bf16[128,8,128]{2,1,0:T(8,128)(2,1)S(1)}, u32[]{:S(2)}, u32[]{:S(2)}) collective-permute-start(bf16[128,8,128]{2,1,0:T(8,128)(2,1)S(1)} %get-tuple-element.81), channel_id=1, source_target_pairs={{0,8},{1,9},{2,10},{3,11},{4,12},{5,13},{6,14},{7,15},{8,16},{9,17... | collective-permute-start | bytes 786440 | tf_op jit(solution)/shard_map/ppermute | solution.py:263
  34.2 2.4 %collective-permute-start.4 = (bf16[128,8,128]{2,1,0:T(8,128)(2,1)S(1)}, bf16[128,8,128]{2,1,0:T(8,128)(2,1)S(1)}, u32[]{:S(2)}, u32[]{:S(2)}) collective-permute-start(bf16[128,8,128]{2,1,0:T(8,128)(2,1)S(1)} %get-tuple-element.82), channel_id=1, source_target_pairs={{0,16},{1,17},{2,18},{3,19},{4,20},{5,21},{6,22},{7,23},{8,24},{9,... | collective-permute-start | bytes 786440 | tf_op jit(solution)/shard_map/ppermute | solution.py:263
  36.6 1.1 collective-permute-start.3
  37.7 1.8 %collective-permute-done.5 = bf16[128,8,128]{2,1,0:T(8,128)(2,1)S(1)} collective-permute-done((bf16[128,8,128]{2,1,0:T(8,128)(2,1)S(1)}, bf16[128,8,128]{2,1,0:T(8,128)(2,1)S(1)}, u32[]{:S(2)}, u32[]{:S(2)}) %collective-permute-start.5) | collective-permute-done | bytes 262176 | tf_op jit(solution)/shard_map/ppermute | solution.py:263
  39.5 4.0 %collective-permute-done.4 = bf16[128,8,128]{2,1,0:T(8,128)(2,1)S(1)} collective-permute-done((bf16[128,8,128]{2,1,0:T(8,128)(2,1)S(1)}, bf16[128,8,128]{2,1,0:T(8,128)(2,1)S(1)}, u32[]{:S(2)}, u32[]{:S(2)}) %collective-permute-start.4) | collective-permute-done | bytes 262176 | tf_op jit(solution)/shard_map/ppermute | solution.py:263
  43.4 0.1 fusion.1
  43.5 3.7 %collective-permute-start.6 = (bf16[128,8,128]{2,1,0:T(8,128)(2,1)S(1)}, bf16[128,8,128]{2,1,0:T(8,128)(2,1)S(1)}, u32[]{:S(2)}, u32[]{:S(2)}) collective-permute-start(bf16[128,8,128]{2,1,0:T(8,128)(2,1)S(1)} %fusion.1), channel_id=1, source_target_pairs={{0,1},{1,0},{2,3},{3,2},{4,5},{5,4},{6,7},{7,6},{8,9},{9,8},{10,11... | collective-permute-start | bytes 786440 | tf_op jit(solution)/shard_map/ppermute | solution.py:266
  47.2 4.2 %collective-permute-done.6 = bf16[128,8,128]{2,1,0:T(8,128)(2,1)S(1)} collective-permute-done((bf16[128,8,128]{2,1,0:T(8,128)(2,1)S(1)}, bf16[128,8,128]{2,1,0:T(8,128)(2,1)S(1)}, u32[]{:S(2)}, u32[]{:S(2)}) %collective-permute-start.6) | collective-permute-done | bytes 262176 | tf_op jit(solution)/shard_map/ppermute | solution.py:266
  51.5 1.5 %collective-permute-start.9 = (bf16[128,8,128]{2,1,0:T(8,128)(2,1)S(1)}, bf16[128,8,128]{2,1,0:T(8,128)(2,1)S(1)}, u32[]{:S(2)}, u32[]{:S(2)}) collective-permute-start(bf16[128,8,128]{2,1,0:T(8,128)(2,1)S(1)} %broadcast_select_fusion), channel_id=1, source_target_pairs={{0,24},{1,25},{2,26},{3,27},{4,28},{5,29},{6,30},{7,31},{8,0},{9,1... | collective-permute-start | bytes 786440 | tf_op jit(solution)/shard_map/ppermute | solution.py:263
  52.9 1.2 collective-permute-start.8
  54.2 0.1 collective-permute-start.7
  54.2 2.5 %collective-permute-done.9 = bf16[128,8,128]{2,1,0:T(8,128)(2,1)S(1)} collective-permute-done((bf16[128,8,128]{2,1,0:T(8,128)(2,1)S(1)}, bf16[128,8,128]{2,1,0:T(8,128)(2,1)S(1)}, u32[]{:S(2)}, u32[]{:S(2)}) %collective-permute-start.9) | collective-permute-done | bytes 262176 | tf_op jit(solution)/shard_map/ppermute | solution.py:263
  56.8 3.0 %collective-permute-done.8 = bf16[128,8,128]{2,1,0:T(8,128)(2,1)S(1)} collective-permute-done((bf16[128,8,128]{2,1,0:T(8,128)(2,1)S(1)}, bf16[128,8,128]{2,1,0:T(8,128)(2,1)S(1)}, u32[]{:S(2)}, u32[]{:S(2)}) %collective-permute-start.8) | collective-permute-done | bytes 262176 | tf_op jit(solution)/shard_map/ppermute | solution.py:263
  59.8 3.0 %collective-permute-done.7 = bf16[128,8,128]{2,1,0:T(8,128)(2,1)S(1)} collective-permute-done((bf16[128,8,128]{2,1,0:T(8,128)(2,1)S(1)}, bf16[128,8,128]{2,1,0:T(8,128)(2,1)S(1)}, u32[]{:S(2)}, u32[]{:S(2)}) %collective-permute-start.7) | collective-permute-done | bytes 262176 | tf_op jit(solution)/shard_map/ppermute | solution.py:263
  62.8 0.1 pad_maximum_fusion
  62.9 2.4 %collective-permute-start.11 = (bf16[4,128,8,128]{3,2,1,0:T(8,128)(2,1)S(1)}, bf16[4,128,8,128]{3,2,1,0:T(8,128)(2,1)S(1)}, u32[]{:S(2)}, u32[]{:S(2)}) collective-permute-start(bf16[4,128,8,128]{3,2,1,0:T(8,128)(2,1)S(1)} %pad_maximum_fusion), channel_id=1, source_target_pairs={{0,6},{1,7},{2,0},{3,1},{4,2},{5,3},{6,4},{7,5},{8,14},{9,15},{10,... | collective-permute-start | bytes 3145736 | tf_op jit(solution)/shard_map/ppermute | solution.py:263
  65.3 12.2 %shard_map.49 = (f32[128,768]{1,0:T(8,128)S(1)}, bf16[128,768]{1,0:T(8,128)(2,1)S(1)}) custom-call(s32[2]{0:T(128)S(1)} %pad_add_fusion.1.place_ref, f32[32,8,3,32,128]{4,3,2,1,0:T(8,128)S(1)} %shard_map.48.r_ref, bf16[8192,768]{1,0:T(8,128)(2,1)S(1)} %shard_map.47.t_ref, bf16[512,8,128]{2,1,0:T(8,128)(2,1)S(1)} %bitcast.41), custom_call_target="tpu_custom_call" | custom-call | flops 9663676416 | bytes 12582912 | tf_op jit(solution)/shard_map/pallas_call | solution.py:197
  77.6 1.1 collective-permute-start.13
  78.7 1.8 %collective-permute-done.10 = bf16[4,128,8,128]{3,2,1,0:T(8,128)(2,1)S(1)} collective-permute-done((bf16[4,128,8,128]{3,2,1,0:T(8,128)(2,1)S(1)}, bf16[4,128,8,128]{3,2,1,0:T(8,128)(2,1)S(1)}, u32[]{:S(2)}, u32[]{:S(2)}) %collective-permute-start.10) | collective-permute-done | bytes 1048608 | tf_op jit(solution)/shard_map/ppermute | solution.py:263
  80.5 0.0 collective-permute-start.12
  80.5 23.0 %shard_map.50 = (f32[256,768]{1,0:T(8,128)S(1)}, bf16[256,768]{1,0:T(8,128)(2,1)S(1)}) custom-call(s32[2]{0:T(128)S(1)} %pad_add_fusion.1.place_ref, f32[32,8,3,32,128]{4,3,2,1,0:T(8,128)S(1)} %shard_map.48.r_ref, bf16[8192,768]{1,0:T(8,128)(2,1)S(1)} %shard_map.47.t_ref, bf16[512,8,128]{2,1,0:T(8,128)(2,1)S(1)} %bitcast.47, bf16[512,8,128]{2,1,0:T(8,128)(2,1)S(1)} %bitcast.46), custom_call_target="tpu_custom_call" | custom-call | flops 19327352832 | bytes 12582912 | tf_op jit(solution)/shard_map/pallas_call | solution.py:197
  103.5 1.1 collective-permute-start.14
  104.6 7.1 %shard_map.51 = bf16[128,768]{1,0:T(8,128)(2,1)S(1)} custom-call(s32[2]{0:T(128)S(1)} %pad_add_fusion.1.place_ref, f32[32,8,3,32,128]{4,3,2,1,0:T(8,128)S(1)} %shard_map.48.r_ref, bf16[8192,768]{1,0:T(8,128)(2,1)S(1)} %shard_map.47.t_ref, bf16[512,8,128]{2,1,0:T(8,128)(2,1)S(1)} %bitcast.39), custom_call_target="tpu_custom_call" | custom-call | flops 4831838208 | bytes 12582912 | tf_op jit(solution)/shard_map/pallas_call | solution.py:197
  111.6 0.5 collective-permute-start.15
  112.2 7.1 %shard_map.52.refs_2_ = f32[128,768]{1,0:T(8,128)S(1)} custom-call(s32[2]{0:T(128)S(1)} %pad_add_fusion.1.place_ref, f32[32,8,3,32,128]{4,3,2,1,0:T(8,128)S(1)} %shard_map.48.r_ref, bf16[8192,768]{1,0:T(8,128)(2,1)S(1)} %shard_map.47.t_ref, bf16[512,8,128]{2,1,0:T(8,128)(2,1)S(1)} %bitcast.40), custom_call_target="tpu_custom_call" | custom-call | flops 4831838208 | bytes 12582912 | tf_op jit(solution)/shard_map/pallas_call | solution.py:197
  119.3 0.7 shard_map.53
  120.0 6.6 %collective-permute-start.16 = (bf16[4,64,768]{2,1,0:T(8,128)(2,1)S(1)}, bf16[4,64,768]{2,1,0:T(8,128)(2,1)S(1)}, u32[]{:S(2)}, u32[]{:S(2)}) collective-permute-start(bf16[4,64,768]{2,1,0:T(8,128)(2,1)S(1)} %get-tuple-element.80), channel_id=1, source_target_pairs={{0,32},{32,0},{64,96},{96,64},{1,33},{33,1},{65,97},{97,65},{2,34}... | collective-permute-start | bytes 1179656 | tf_op jit(solution)/shard_map/ppermute | solution.py:337
  126.6 1.3 %collective-permute-done.16 = bf16[4,64,768]{2,1,0:T(8,128)(2,1)S(1)} collective-permute-done((bf16[4,64,768]{2,1,0:T(8,128)(2,1)S(1)}, bf16[4,64,768]{2,1,0:T(8,128)(2,1)S(1)}, u32[]{:S(2)}, u32[]{:S(2)}) %collective-permute-start.16) | collective-permute-done | bytes 393248 | tf_op jit(solution)/shard_map/ppermute | solution.py:337
  127.9 0.1 convert_add_fusion
  128.0 0.9 copy.5
  (12 shorter events, 0.1 us)
Async XLA Ops:
  1.7 2.2 %copy-start = (bf16[8,2,32,4096]{3,2,1,0:T(8,128)(2,1)S(1)}, bf16[8,2,32,4096]{3,2,1,0:T(8,128)(2,1)}, u32[]{:S(2)}) copy-start(bf16[8,2,32,4096]{3,2,1,0:T(8,128)(2,1)} %s_hbm.1) | copy-start | bytes 12582916
  4.6 16.2 %collective-permute-start.1 = (bf16[4,128,8,128]{3,2,1,0:T(8,128)(2,1)S(1)}, bf16[4,128,8,128]{3,2,1,0:T(8,128)(2,1)S(1)}, u32[]{:S(2)}, u32[]{:S(2)}) collective-permute-start(bf16[4,128,8,128]{3,2,1,0:T(8,128)(2,1)S(1)} %bitcast.45), channel_id=1, source_target_pairs={{0,4},{1,5},{2,6},{3,7},{4,0},{5,1},{6,2},{7,3},{8,12},{9,13},{10,... | collective-permute-start | bytes 3145736 | tf_op jit(solution)/shard_map/ppermute | solution.py:263
  8.2 24.1 %collective-permute-start = (bf16[4,128,8,128]{3,2,1,0:T(8,128)(2,1)S(1)}, bf16[4,128,8,128]{3,2,1,0:T(8,128)(2,1)S(1)}, u32[]{:S(2)}, u32[]{:S(2)}) collective-permute-start(bf16[4,128,8,128]{3,2,1,0:T(8,128)(2,1)S(1)} %bitcast.44), channel_id=1, source_target_pairs={{0,6},{1,7},{2,0},{3,1},{4,2},{5,3},{6,4},{7,5},{8,14},{9,15},{10,... | collective-permute-start | bytes 3145736 | tf_op jit(solution)/shard_map/ppermute | solution.py:263
  9.1 23.2 %collective-permute-start.2 = (bf16[4,128,8,128]{3,2,1,0:T(8,128)(2,1)S(1)}, bf16[4,128,8,128]{3,2,1,0:T(8,128)(2,1)S(1)}, u32[]{:S(2)}, u32[]{:S(2)}) collective-permute-start(bf16[4,128,8,128]{3,2,1,0:T(8,128)(2,1)S(1)} %bitcast.43), channel_id=1, source_target_pairs={{0,2},{1,3},{2,4},{3,5},{4,6},{5,7},{6,0},{7,1},{8,10},{9,11},{10,... | collective-permute-start | bytes 3145736 | tf_op jit(solution)/shard_map/ppermute | solution.py:263
  9.7 2.2 %copy-start.1 = (bf16[8,2,32,4096]{3,2,1,0:T(8,128)(2,1)S(1)}, bf16[8,2,32,4096]{3,2,1,0:T(8,128)(2,1)}, u32[]{:S(2)}) copy-start(bf16[8,2,32,4096]{3,2,1,0:T(8,128)(2,1)} %r_ref.1) | copy-start | bytes 12582916
  32.6 6.9 %collective-permute-start.5 = (bf16[128,8,128]{2,1,0:T(8,128)(2,1)S(1)}, bf16[128,8,128]{2,1,0:T(8,128)(2,1)S(1)}, u32[]{:S(2)}, u32[]{:S(2)}) collective-permute-start(bf16[128,8,128]{2,1,0:T(8,128)(2,1)S(1)} %get-tuple-element.81), channel_id=1, source_target_pairs={{0,8},{1,9},{2,10},{3,11},{4,12},{5,13},{6,14},{7,15},{8,16},{9,17... | collective-permute-start | bytes 786440 | tf_op jit(solution)/shard_map/ppermute | solution.py:263
  34.2 9.3 %collective-permute-start.4 = (bf16[128,8,128]{2,1,0:T(8,128)(2,1)S(1)}, bf16[128,8,128]{2,1,0:T(8,128)(2,1)S(1)}, u32[]{:S(2)}, u32[]{:S(2)}) collective-permute-start(bf16[128,8,128]{2,1,0:T(8,128)(2,1)S(1)} %get-tuple-element.82), channel_id=1, source_target_pairs={{0,16},{1,17},{2,18},{3,19},{4,20},{5,21},{6,22},{7,23},{8,24},{9,... | collective-permute-start | bytes 786440 | tf_op jit(solution)/shard_map/ppermute | solution.py:263
  36.6 6.9 %collective-permute-start.3 = (bf16[128,8,128]{2,1,0:T(8,128)(2,1)S(1)}, bf16[128,8,128]{2,1,0:T(8,128)(2,1)S(1)}, u32[]{:S(2)}, u32[]{:S(2)}) collective-permute-start(bf16[128,8,128]{2,1,0:T(8,128)(2,1)S(1)} %get-tuple-element.83), channel_id=1, source_target_pairs={{0,24},{1,25},{2,26},{3,27},{4,28},{5,29},{6,30},{7,31},{8,0},{9,1... | collective-permute-start | bytes 786440 | tf_op jit(solution)/shard_map/ppermute | solution.py:263
  43.5 7.9 %collective-permute-start.6 = (bf16[128,8,128]{2,1,0:T(8,128)(2,1)S(1)}, bf16[128,8,128]{2,1,0:T(8,128)(2,1)S(1)}, u32[]{:S(2)}, u32[]{:S(2)}) collective-permute-start(bf16[128,8,128]{2,1,0:T(8,128)(2,1)S(1)} %fusion.1), channel_id=1, source_target_pairs={{0,1},{1,0},{2,3},{3,2},{4,5},{5,4},{6,7},{7,6},{8,9},{9,8},{10,11... | collective-permute-start | bytes 786440 | tf_op jit(solution)/shard_map/ppermute | solution.py:266
  51.5 5.3 %collective-permute-start.9 = (bf16[128,8,128]{2,1,0:T(8,128)(2,1)S(1)}, bf16[128,8,128]{2,1,0:T(8,128)(2,1)S(1)}, u32[]{:S(2)}, u32[]{:S(2)}) collective-permute-start(bf16[128,8,128]{2,1,0:T(8,128)(2,1)S(1)} %broadcast_select_fusion), channel_id=1, source_target_pairs={{0,24},{1,25},{2,26},{3,27},{4,28},{5,29},{6,30},{7,31},{8,0},{9,1... | collective-permute-start | bytes 786440 | tf_op jit(solution)/shard_map/ppermute | solution.py:263
  52.9 6.8 %collective-permute-start.8 = (bf16[128,8,128]{2,1,0:T(8,128)(2,1)S(1)}, bf16[128,8,128]{2,1,0:T(8,128)(2,1)S(1)}, u32[]{:S(2)}, u32[]{:S(2)}) collective-permute-start(bf16[128,8,128]{2,1,0:T(8,128)(2,1)S(1)} %broadcast_select_fusion), channel_id=1, source_target_pairs={{0,16},{1,17},{2,18},{3,19},{4,20},{5,21},{6,22},{7,23},{8,24},{9,... | collective-permute-start | bytes 786440 | tf_op jit(solution)/shard_map/ppermute | solution.py:263
  54.2 8.6 %collective-permute-start.7 = (bf16[128,8,128]{2,1,0:T(8,128)(2,1)S(1)}, bf16[128,8,128]{2,1,0:T(8,128)(2,1)S(1)}, u32[]{:S(2)}, u32[]{:S(2)}) collective-permute-start(bf16[128,8,128]{2,1,0:T(8,128)(2,1)S(1)} %broadcast_select_fusion), channel_id=1, source_target_pairs={{0,8},{1,9},{2,10},{3,11},{4,12},{5,13},{6,14},{7,15},{8,16},{9,17... | collective-permute-start | bytes 786440 | tf_op jit(solution)/shard_map/ppermute | solution.py:263
  62.9 15.7 %collective-permute-start.11 = (bf16[4,128,8,128]{3,2,1,0:T(8,128)(2,1)S(1)}, bf16[4,128,8,128]{3,2,1,0:T(8,128)(2,1)S(1)}, u32[]{:S(2)}, u32[]{:S(2)}) collective-permute-start(bf16[4,128,8,128]{3,2,1,0:T(8,128)(2,1)S(1)} %pad_maximum_fusion), channel_id=1, source_target_pairs={{0,6},{1,7},{2,0},{3,1},{4,2},{5,3},{6,4},{7,5},{8,14},{9,15},{10,... | collective-permute-start | bytes 3145736 | tf_op jit(solution)/shard_map/ppermute | solution.py:263
  65.3 15.2 %collective-permute-start.10 = (bf16[4,128,8,128]{3,2,1,0:T(8,128)(2,1)S(1)}, bf16[4,128,8,128]{3,2,1,0:T(8,128)(2,1)S(1)}, u32[]{:S(2)}, u32[]{:S(2)}) collective-permute-start(bf16[4,128,8,128]{3,2,1,0:T(8,128)(2,1)S(1)} %pad_maximum_fusion), channel_id=1, source_target_pairs={{0,2},{1,3},{2,4},{3,5},{4,6},{5,7},{6,0},{7,1},{8,10},{9,11},{10,... | collective-permute-start | bytes 3145736 | tf_op jit(solution)/shard_map/ppermute | solution.py:263
  77.6 41.7 %collective-permute-start.13 = (bf16[128,768]{1,0:T(8,128)(2,1)S(1)}, bf16[128,768]{1,0:T(8,128)(2,1)S(1)}, u32[]{:S(2)}, u32[]{:S(2)}) collective-permute-start(bf16[128,768]{1,0:T(8,128)(2,1)S(1)} %get-tuple-element.76), channel_id=1, source_target_pairs={{0,64},{64,0},{32,96},{96,32},{1,65},{65,1},{33,97},{97,33},{2,66}... | collective-permute-start | bytes 589832 | tf_op jit(solution)/shard_map/ppermute | solution.py:335
  80.5 24.1 %collective-permute-start.12 = (bf16[4,128,8,128]{3,2,1,0:T(8,128)(2,1)S(1)}, bf16[4,128,8,128]{3,2,1,0:T(8,128)(2,1)S(1)}, u32[]{:S(2)}, u32[]{:S(2)}) collective-permute-start(bf16[4,128,8,128]{3,2,1,0:T(8,128)(2,1)S(1)} %pad_maximum_fusion), channel_id=1, source_target_pairs={{0,4},{1,5},{2,6},{3,7},{4,0},{5,1},{6,2},{7,3},{8,12},{9,13},{10,... | collective-permute-start | bytes 3145736 | tf_op jit(solution)/shard_map/ppermute | solution.py:263
  103.5 15.8 %collective-permute-start.14 = (bf16[256,768]{1,0:T(8,128)(2,1)S(1)}, bf16[256,768]{1,0:T(8,128)(2,1)S(1)}, u32[]{:S(2)}, u32[]{:S(2)}) collective-permute-start(bf16[256,768]{1,0:T(8,128)(2,1)S(1)} %get-tuple-element.77), channel_id=1, source_target_pairs={{0,64},{64,0},{32,96},{96,32},{1,65},{65,1},{33,97},{97,33},{2,66}... | collective-permute-start | bytes 1179656 | tf_op jit(solution)/shard_map/ppermute | solution.py:335
  111.6 7.6 %collective-permute-start.15 = (bf16[128,768]{1,0:T(8,128)(2,1)S(1)}, bf16[128,768]{1,0:T(8,128)(2,1)S(1)}, u32[]{:S(2)}, u32[]{:S(2)}) collective-permute-start(bf16[128,768]{1,0:T(8,128)(2,1)S(1)} %shard_map.51), channel_id=1, source_target_pairs={{0,64},{64,0},{32,96},{96,32},{1,65},{65,1},{33,97},{97,33},{2,66}... | collective-permute-start | bytes 589832 | tf_op jit(solution)/shard_map/ppermute | solution.py:335
  120.0 8.0 %collective-permute-start.16 = (bf16[4,64,768]{2,1,0:T(8,128)(2,1)S(1)}, bf16[4,64,768]{2,1,0:T(8,128)(2,1)S(1)}, u32[]{:S(2)}, u32[]{:S(2)}) collective-permute-start(bf16[4,64,768]{2,1,0:T(8,128)(2,1)S(1)} %get-tuple-element.80), channel_id=1, source_target_pairs={{0,32},{32,0},{64,96},{96,64},{1,33},{33,1},{65,97},{97,65},{2,34}... | collective-permute-start | bytes 1179656 | tf_op jit(solution)/shard_map/ppermute | solution.py:337

commit v3 on v2

--- a/solution.py
+++ b/solution.py
@@ -54,35 +54,27 @@
     )(*tables)
 
 
-def cut_sources(sources, flags, place):
+def cut_sources(sources, flags, place, wanted):
     windows, parts, channels, bins = sources.shape
     columns = bins // LANES
     wide = columns // QUARTERS
     total = windows * parts * columns
 
-    def kernel(place_ref, s_hbm, f_ref, *refs):
-        outs = refs[:QUARTERS]
-        held, rows, sems = refs[QUARTERS:]
+    def kernel(place_ref, s_ref, f_ref, *refs):
+        outs, rows = refs[:-1], refs[-1]
 
         @pl.when(place_ref[0] == 1)
         def _():
-            def fetch(w):
-                return pltpu.make_async_copy(s_hbm.at[w], held.at[w], sems.at[w])
-
-            for w in range(windows):
-                fetch(w).start()
-
             def one(w, carry):
-                fetch(w).wait()
                 for c in range(parts):
                     for column in range(columns):
                         lanes = slice(column * LANES, (column + 1) * LANES)
-                        rows[column] = held[w, c, :, lanes].astype(jnp.float32) * f_ref[w]
-                    for d in range(QUARTERS):
+                        rows[c, column] = s_ref[w, c, :, lanes].astype(jnp.float32) * f_ref[w]
+                    for d, out in zip(wanted, outs):
                         m = lax.rem(place_ref[1] + d, QUARTERS)
                         for column in range(columns):
                             spot = ((column // wide) * windows * parts + w * parts + c) * wide + column % wide
-                            outs[d][spot] = rows[column, pl.ds(m, ROWS, stride=QUARTERS)].astype(jnp.bfloat16)
+                            out[spot] = rows[c, column, pl.ds(m, ROWS, stride=QUARTERS)].astype(jnp.bfloat16)
                 return carry
 
             lax.fori_loop(0, windows, one, 0)
@@ -90,15 +82,11 @@
     in_vmem = pl.BlockSpec(memory_space=pltpu.VMEM)
     return pl.pallas_call(
         kernel,
-        in_specs=[pl.BlockSpec(memory_space=pltpu.SMEM), pl.BlockSpec(memory_space=pl.ANY), in_vmem],
-        out_specs=[in_vmem] * QUARTERS,
-        scratch_shapes=[
-            pltpu.VMEM(sources.shape, jnp.bfloat16),
-            pltpu.VMEM((columns, channels, LANES), jnp.float32),
-            pltpu.SemaphoreType.DMA((windows,)),
-        ],
-        out_shape=[jax.ShapeDtypeStruct((total, ROWS, LANES), jnp.bfloat16)] * QUARTERS,
-        compiler_params=pltpu.CompilerParams(vmem_limit_bytes=16 * MIB),
+        in_specs=[pl.BlockSpec(memory_space=pltpu.SMEM), in_vmem, in_vmem],
+        out_specs=[in_vmem] * len(wanted),
+        scratch_shapes=[pltpu.VMEM((parts, columns, channels, LANES), jnp.float32)],
+        out_shape=[jax.ShapeDtypeStruct((total, ROWS, LANES), jnp.bfloat16)] * len(wanted),
+        compiler_params=pltpu.CompilerParams(vmem_limit_bytes=8 * MIB),
         cost_estimate=pl.CostEstimate(flops=2 * sources.size, bytes_accessed=4 * sources.size, transcendentals=0),
     )(place, sources, flags)
 
@@ -131,32 +119,47 @@
     )(spectra, flags)
 
 
-def lag_quarters(receiving, tiles, table, place, side=None):
+def lag_quarters(receiving, tiles, table, place, side=None, nears=None, before=None):
     columns, windows, _, receivers, _ = receiving.shape
     parts = 2
     bins = columns * LANES
-    total = tiles[0].shape[0]
     number = len(tiles)
     doubled, lags = table.shape
     wide = columns // QUARTERS
     half = ROWS * receivers // 2
+    piece = windows * parts * wide
+    count = columns if nears is None else wide * len(nears)
+    added = 0 if before is None else 1
 
     sides = (0, 1) if side is None else (side,)
     shapes = [
         jax.ShapeDtypeStruct((number * half, lags), jnp.float32),
         jax.ShapeDtypeStruct((number * half, lags), jnp.bfloat16),
     ]
+    outputs = [shapes[i] for i in sides]
+    if nears is not None and before is None:
+        outputs = [jax.ShapeDtypeStruct((2 * number * half, lags), jnp.float32)]
 
     def kernel(place_ref, r_ref, t_ref, *refs):
-        outs = refs[number : number + len(sides)]
-        sf, cross = refs[number + len(sides) :]
+        outs = refs[number + added : number + added + len(outputs)]
+        sf, cross = refs[number + added + len(outputs) :]
         chip = place_ref[1]
 
-        def one(column, carry):
-            near = lax.rem(place_ref[0] + QUARTERS - column // wide, QUARTERS)
-            base = near * (total // QUARTERS) + lax.rem(column, wide)
-            to_real = pl.ds(pl.multiple_of(column * LANES, LANES), LANES)
-            to_imag = pl.ds(pl.multiple_of(bins + column * LANES, LANES), LANES)
+        def one(i, carry):
+            if nears is None:
+                column = i
+                near = lax.rem(place_ref[0] + QUARTERS - column // wide, QUARTERS)
+                base = near * piece + lax.rem(column, wide)
+                real_column, imag_column = column, columns + column
+            else:
+                turn = i // wide
+                quarter = lax.rem(place_ref[0] + QUARTERS - nears[0] - turn, QUARTERS)
+                column = quarter * wide + lax.rem(i, wide)
+                base = (nears[0] + turn) * piece + lax.rem(i, wide)
+                real_column = turn * 2 * wide + lax.rem(i, wide)
+                imag_column = real_column + wide
+            to_real = pl.ds(pl.multiple_of(real_column * LANES, LANES), LANES)
+            to_imag = pl.ds(pl.multiple_of(imag_column * LANES, LANES), LANES)
             for q in range(number):
                 for w in range(windows):
                     real = refs[q][base + w * parts * wide].astype(jnp.float32)
@@ -186,28 +189,40 @@
                             cross[row, to_imag] = (third - first + second).astype(jnp.bfloat16)
             return carry
 
-        lax.fori_loop(0, columns, one, 0)
+        lax.fori_loop(0, count, one, 0)
         for n in range(0, lags, WIDE):
             part = slice(n, n + WIDE)
-            value = jnp.dot(cross[...], t_ref[:, part], preferred_element_type=jnp.float32)
+            if nears is None:
+                value = jnp.dot(cross[...], t_ref[:, part], preferred_element_type=jnp.float32)
+            else:
+                value = None if before is None else refs[number][:, part]
+                span = wide * LANES
+                for j in range(2 * len(nears)):
+                    quarter = lax.rem(place_ref[0] + QUARTERS - nears[j // 2], QUARTERS)
+                    some = pl.ds(pl.multiple_of(j % 2 * bins + quarter * span, span), span)
+                    term = jnp.dot(
+                        cross[:, j * span : (j + 1) * span], t_ref[some, part], preferred_element_type=jnp.float32
+                    )
+                    value = term if value is None else value + term
             for i, out in enumerate(outs):
-                out[:, part] = value[i * number * half : (i + 1) * number * half].astype(out.dtype)
-
-    in_vmem = pl.BlockSpec(memory_space=pltpu.VMEM)
-    return pl.pallas_call(
-        kernel,
-        in_specs=[pl.BlockSpec(memory_space=pltpu.SMEM)] + [in_vmem] * (2 + number),
-        out_specs=[in_vmem] * len(sides),
+                rows = number * half if len(outs) == len(sides) else 2 * number * half
+                out[:, part] = value[i * rows : (i + 1) * rows].astype(out.dtype)
+
+    in_vmem = pl.BlockSpec(memory_space=pltpu.VMEM)
+    return pl.pallas_call(
+        kernel,
+        in_specs=[pl.BlockSpec(memory_space=pltpu.SMEM)] + [in_vmem] * (2 + number + added),
+        out_specs=[in_vmem] * len(outputs),
         scratch_shapes=[
             pltpu.VMEM((number, windows, 3, 4 * len(sides), LANES), jnp.float32),
-            pltpu.VMEM((len(sides) * number * half, doubled), jnp.bfloat16),
+            pltpu.VMEM((len(sides) * number * half, 2 * count * LANES), jnp.bfloat16),
         ],
-        out_shape=[shapes[i] for i in sides],
+        out_shape=outputs,
         compiler_params=pltpu.CompilerParams(vmem_limit_bytes=LIMIT * MIB),
         cost_estimate=pl.CostEstimate(
-            flops=len(sides) * number * half * 2 * doubled * lags * 3, bytes_accessed=2 * table.size, transcendentals=0
+            flops=len(sides) * number * half * 4 * count * LANES * lags * 3, bytes_accessed=2 * table.size, transcendentals=0
         ),
-    )(place, receiving, table, *tiles)
+    )(place, receiving, table, *tiles, *([before] if added else []))
 
 
 def split_cores(kept, received, groups, place):
@@ -267,8 +282,8 @@
 
     @staticmethod
     def place(index, core):
-        x, y = index // 8, (index // 2) % 4
-        return jnp.where(core == 0, x, y), jnp.where(core == 0, y, x), index % 2
+        x, y = index >> 3, (index >> 1) & 3
+        return jnp.where(core == 0, x, y), jnp.where(core == 0, y, x), index & 1
 
 
 def pick(values, chosen):
@@ -288,16 +303,16 @@
     steps = range(1, QUARTERS)
     owner = owners[0].astype(jnp.int32)
     win = lax.axis_index("win")
-    chip, core = win // 2, win % 2
+    chip, core = win >> 1, win & 1
     rcv = lax.axis_index("rcv")
     u, v, z = grid.place(rcv, core)
     owner_u, owner_v, owner_z = grid.place(owner, core)
     cut_place = jnp.stack([(rcv == owner).astype(jnp.int32), v])
     lag_place = jnp.stack([u, chip])
     end_place = jnp.stack([v, core])
-    to_bins = [((u + d) % QUARTERS).astype(jnp.uint32) for d in range(QUARTERS)]
-    off_v = [(v - owner_v) % QUARTERS == d for d in steps]
-    off_u = [(u - owner_u) % QUARTERS == d for d in steps]
+    to_bins = [((u + d) & 3).astype(jnp.uint32) for d in range(QUARTERS)]
+    off_v = [(v - owner_v) & 3 == d for d in steps]
+    off_u = [(u - owner_u) & 3 == d for d in steps]
     same_z = z == owner_z
     scalars = (cut_place, lag_place, end_place, to_bins, off_v, off_u, same_z)
     scalars, usable = lax.optimization_barrier((scalars, usable))
@@ -307,7 +322,9 @@
     table = build_table(bins, LAGS, windows * lax.axis_size("win"))
     receiving = mask_receivers(spectra, flags)
     tiles = windows * parts * (bins // LANES)
-    cut = cut_sources(sources, flags, cut_place)
+    cut = cut_sources(sources, flags, cut_place, (1, 2, 3))
+    own = cut_sources(sources, flags, cut_place, (0,))
+    cut = own + cut
     cut = [part.reshape(QUARTERS, tiles // QUARTERS, ROWS, LANES) for part in cut]
     dealt = [cut[0]] + [grid.move(cut[d], 1, d) for d in steps]
     mine = pick(dealt, off_v)
@@ -315,7 +332,10 @@
     dealt = [at(mine, to_bins[0])] + [grid.move(at(mine, to_bins[d]), 0, d) for d in steps]
     mine = pick(dealt, off_u)
     mine = jnp.where(same_z, mine, grid.flip(mine))
-    row = jnp.stack([mine] + [grid.move(mine, 0, d) for d in steps])
+    near = [mine] + [grid.move(mine, 0, d) for d in steps]
+    (early,) = lag_quarters(receiving, [mine], table, lag_place, nears=(0,))
+    near, early = lax.optimization_barrier((near, early))
+    row = jnp.stack(near)
     quarters = [row, grid.move(row, 1, 1), None, grid.move(row, 1, 3)]
 
     kept, received = [], []
@@ -324,7 +344,9 @@
             row, quarters[1], quarters[3] = lax.optimization_barrier((row, quarters[1], quarters[3]))
             quarters[2] = grid.move(row, 1, 2)
         blocks = [quarters[d].reshape(tiles, ROWS, LANES) for d in group]
-        if group != GROUPS[-1]:
+        if group == GROUPS[0]:
+            mine, given = lag_quarters(receiving, blocks, table, lag_place, nears=(1, 2, 3), before=early)
+        elif group != GROUPS[-1]:
             mine, given = lag_quarters(receiving, blocks, table, lag_place)
         else:
             (given,) = lag_quarters(receiving, blocks, table, lag_place, 1)

time: 130 us -> 129 us (level)
  local copies, waits for them, and re-layouts: 5.46 us -> 3.27 us
    unnamed x4, local copies, waits for them, and re-layouts: 4.37 us -> 2.19 us
    pallas_call x4 -> x5, Pallas kernels: 49.3 us -> 50 us  [lag_quarters(): pl.pallas_call(kernel, in_specs=[pl.BlockSpec(memory_space=pltpu.SMEM)] +...]
  transfers between devices with their start and end apart: 17 -> 17, of which waited for: 10 -> 10; matrix products, arithmetic and copies ran while one was open for 1% -> 1% of each run, Pallas kernels for 43% -> 44%
where the time goes in v3:
time: 129 us
  Pallas kernels  57.4 us (44%)
  waiting for transfers between devices  35.8 us (28%)
  starting transfers between devices  28.3 us (22%)
  local copies, waits for them, and re-layouts  3.27 us (3%)
  other arithmetic  2.98 us (2%)
    pallas_call x5, Pallas kernels, lag_quarters(): pl.pallas_call(kernel, in_specs=[pl.BlockSpec(memory_space=pltpu.SMEM)] +...  50 us
    ppermute x12, waiting for transfers between devices, move(): return lax.ppermute(value, ('win', 'rcv'), self.pairs[axis, step])  30.3 us
    ppermute x12, starting transfers between devices, move(): return lax.ppermute(value, ('win', 'rcv'), self.pairs[axis, step])  15.4 us
    ppermute x1, starting transfers between devices, local(): lax.ppermute(given, 'win', [(0, 1), (1, 0), (2, 3), (3, 2)])  6.54 us
    ppermute x1, waiting for transfers between devices, flip(): return lax.ppermute(value, 'rcv', [(i, i ^ 1) for i in range(32)])  4.23 us
    pallas_call x1, Pallas kernels, build_table(): pl.pallas_call(kernel, in_specs=[in_vmem] * 4, out_specs=in_vmem, out_sha...  4.21 us
    ppermute x1, starting transfers between devices, flip(): return lax.ppermute(value, 'rcv', [(i, i ^ 1) for i in range(32)])  3.68 us
    ppermute x3, starting transfers between devices, local(): lax.ppermute(given, 'win', [(0, 2), (2, 0), (1, 3), (3, 1)])  2.71 us
  transfers between devices with their start and end apart: 17, of which 10 were waited for; matrix products, arithmetic and copies ran while one was open for 1% of the time, Pallas kernels for 44%

profile of v3, /device:TPU:1, one launch (start us, length us, event | category | flops | bytes accessed | tf_op | source)
XLA Modules:
  0.0 128.7 jit_solution(10012095537920098098)
XLA Ops:
  0.7 0.1 pad_add_fusion.1.place_ref
  0.8 0.1 pad_add_fusion
  0.8 0.7 convert_element_type.33
  1.5 0.1 broadcast_in_dim.2.f_ref
  1.6 0.0 copy-start
  1.6 2.2 %copy-done = bf16[8,2,32,4096]{3,2,1,0:T(8,128)(2,1)S(1)} copy-done((bf16[8,2,32,4096]{3,2,1,0:T(8,128)(2,1)S(1)}, bf16[8,2,32,4096]{3,2,1,0:T(8,128)(2,1)}, u32[]{:S(2)}) %copy-start) | copy-done | bytes 4194328
  3.8 0.5 shard_map.46
  4.4 3.7 %collective-permute-start.1 = (bf16[4,128,8,128]{3,2,1,0:T(8,128)(2,1)S(1)}, bf16[4,128,8,128]{3,2,1,0:T(8,128)(2,1)S(1)}, u32[]{:S(2)}, u32[]{:S(2)}) collective-permute-start(bf16[4,128,8,128]{3,2,1,0:T(8,128)(2,1)S(1)} %bitcast.45), channel_id=1, source_target_pairs={{0,4},{1,5},{2,6},{3,7},{4,0},{5,1},{6,2},{7,3},{8,12},{9,13},{10,... | collective-permute-start | bytes 3145736 | tf_op jit(solution)/shard_map/ppermute | solution.py:278
  8.0 0.9 collective-permute-start
  8.9 0.6 collective-permute-start.2
  9.5 0.5 shard_map.47
  10.1 1.4 %shard_map.49.r_ref = f32[32,8,3,32,128]{4,3,2,1,0:T(8,128)S(1)} custom-call(bf16[8,2,32,4096]{3,2,1,0:T(8,128)(2,1)S(1)} %copy-done.1, f32[8,32,128]{2,1,0:T(8,128)S(1)} %broadcast_in_dim.2.f_ref), custom_call_target="tpu_custom_call" | custom-call | flops 8388608 | bytes 16777216 | tf_op jit(solution)/shard_map/pallas_call | solution.py:112
  11.5 1.6 %fusion.11 = (f32[64,768]{1,0:T(8,128)S(1)}, f32[64,768]{1,0:T(8,128)S(1)}, f32[64,768]{1,0:T(8,128)S(1)}, f32[64,768]{1,0:T(8,128)S(1)}) fusion(s32[768]{0:T(1024)S(1)} %iota_add_fusion, s32[64]{0:T(128)S(1)} %iota_multiply_fusion), kind=kLoop, calls=%fused_computation.29 | loop fusion | flops 1474560 | bytes 789760 | tf_op jit(solution)/shard_map/sin | solution.py:30
  13.1 4.2 %shard_map.48.t_ref = bf16[8192,768]{1,0:T(8,128)(2,1)S(1)} custom-call(f32[64,768]{1,0:T(8,128)S(1)} %get-tuple-element.95.cos_low, f32[64,768]{1,0:T(8,128)S(1)} %get-tuple-element.94.sin_low, f32[64,768]{1,0:T(8,128)S(1)} %get-tuple-element.93.cos_high, f32[64,768]{1,0:T(8,128)S(1)} %get-tuple-element.92.sin_high), custom_call_target="tpu_custom_call" | custom-call | flops 50331648 | bytes 12582912 | tf_op jit(solution)/shard_map/pallas_call | solution.py:47
  17.3 3.2 %collective-permute-done.1 = bf16[4,128,8,128]{3,2,1,0:T(8,128)(2,1)S(1)} collective-permute-done((bf16[4,128,8,128]{3,2,1,0:T(8,128)(2,1)S(1)}, bf16[4,128,8,128]{3,2,1,0:T(8,128)(2,1)S(1)}, u32[]{:S(2)}, u32[]{:S(2)}) %collective-permute-start.1) | collective-permute-done | bytes 1048608 | tf_op jit(solution)/shard_map/ppermute | solution.py:278
  20.6 11.5 %collective-permute-done = bf16[4,128,8,128]{3,2,1,0:T(8,128)(2,1)S(1)} collective-permute-done((bf16[4,128,8,128]{3,2,1,0:T(8,128)(2,1)S(1)}, bf16[4,128,8,128]{3,2,1,0:T(8,128)(2,1)S(1)}, u32[]{:S(2)}, u32[]{:S(2)}) %collective-permute-start) | collective-permute-done | bytes 1048608 | tf_op jit(solution)/shard_map/ppermute | solution.py:278
  32.1 0.2 select_select_fusion
  32.3 0.1 dynamic-slice_bitcast_fusion
  32.4 2.2 %collective-permute-start.5 = (bf16[128,8,128]{2,1,0:T(8,128)(2,1)S(1)}, bf16[128,8,128]{2,1,0:T(8,128)(2,1)S(1)}, u32[]{:S(2)}, u32[]{:S(2)}) collective-permute-start(bf16[128,8,128]{2,1,0:T(8,128)(2,1)S(1)} %get-tuple-element.89), channel_id=1, source_target_pairs={{0,8},{1,9},{2,10},{3,11},{4,12},{5,13},{6,14},{7,15},{8,16},{9,17... | collective-permute-start | bytes 786440 | tf_op jit(solution)/shard_map/ppermute | solution.py:278
  34.6 1.7 %collective-permute-start.4 = (bf16[128,8,128]{2,1,0:T(8,128)(2,1)S(1)}, bf16[128,8,128]{2,1,0:T(8,128)(2,1)S(1)}, u32[]{:S(2)}, u32[]{:S(2)}) collective-permute-start(bf16[128,8,128]{2,1,0:T(8,128)(2,1)S(1)} %get-tuple-element.90), channel_id=1, source_target_pairs={{0,16},{1,17},{2,18},{3,19},{4,20},{5,21},{6,22},{7,23},{8,24},{9,... | collective-permute-start | bytes 786440 | tf_op jit(solution)/shard_map/ppermute | solution.py:278
  36.4 1.1 collective-permute-start.3
  37.5 1.8 %collective-permute-done.5 = bf16[128,8,128]{2,1,0:T(8,128)(2,1)S(1)} collective-permute-done((bf16[128,8,128]{2,1,0:T(8,128)(2,1)S(1)}, bf16[128,8,128]{2,1,0:T(8,128)(2,1)S(1)}, u32[]{:S(2)}, u32[]{:S(2)}) %collective-permute-start.5) | collective-permute-done | bytes 262176 | tf_op jit(solution)/shard_map/ppermute | solution.py:278
  39.3 4.0 %collective-permute-done.4 = bf16[128,8,128]{2,1,0:T(8,128)(2,1)S(1)} collective-permute-done((bf16[128,8,128]{2,1,0:T(8,128)(2,1)S(1)}, bf16[128,8,128]{2,1,0:T(8,128)(2,1)S(1)}, u32[]{:S(2)}, u32[]{:S(2)}) %collective-permute-start.4) | collective-permute-done | bytes 262176 | tf_op jit(solution)/shard_map/ppermute | solution.py:278
  43.2 0.1 fusion.1
  43.3 3.7 %collective-permute-start.6 = (bf16[128,8,128]{2,1,0:T(8,128)(2,1)S(1)}, bf16[128,8,128]{2,1,0:T(8,128)(2,1)S(1)}, u32[]{:S(2)}, u32[]{:S(2)}) collective-permute-start(bf16[128,8,128]{2,1,0:T(8,128)(2,1)S(1)} %fusion.1), channel_id=1, source_target_pairs={{0,1},{1,0},{2,3},{3,2},{4,5},{5,4},{6,7},{7,6},{8,9},{9,8},{10,11... | collective-permute-start | bytes 786440 | tf_op jit(solution)/shard_map/ppermute | solution.py:281
  47.0 4.2 %collective-permute-done.6 = bf16[128,8,128]{2,1,0:T(8,128)(2,1)S(1)} collective-permute-done((bf16[128,8,128]{2,1,0:T(8,128)(2,1)S(1)}, bf16[128,8,128]{2,1,0:T(8,128)(2,1)S(1)}, u32[]{:S(2)}, u32[]{:S(2)}) %collective-permute-start.6) | collective-permute-done | bytes 262176 | tf_op jit(solution)/shard_map/ppermute | solution.py:281
  51.3 1.5 %collective-permute-start.9 = (bf16[128,8,128]{2,1,0:T(8,128)(2,1)S(1)}, bf16[128,8,128]{2,1,0:T(8,128)(2,1)S(1)}, u32[]{:S(2)}, u32[]{:S(2)}) collective-permute-start(bf16[128,8,128]{2,1,0:T(8,128)(2,1)S(1)} %broadcast_select_fusion.refs_0_), channel_id=1, source_target_pairs={{0,24},{1,25},{2,26},{3,27},{4,28},{5,29},{6,30},{7,31},{8,0},{9,1... | collective-permute-start | bytes 786440 | tf_op jit(solution)/shard_map/ppermute | solution.py:278
  52.7 1.2 collective-permute-start.8
  54.0 0.1 collective-permute-start.7
  54.0 3.6 %shard_map.50.refs_1_ = f32[256,768]{1,0:T(8,128)S(1)} custom-call(s32[2]{0:T(128)S(1)} %pad_add_fusion.1.place_ref, f32[32,8,3,32,128]{4,3,2,1,0:T(8,128)S(1)} %shard_map.49.r_ref, bf16[8192,768]{1,0:T(8,128)(2,1)S(1)} %shard_map.48.t_ref, bf16[128,8,128]{2,1,0:T(8,128)(2,1)S(1)} %broadcast_select_fusion.refs_0_), custom_call_target="tpu_custom_call" | custom-call | flops 2415919104 | bytes 12582912 | tf_op jit(solution)/shard_map/pallas_call | solution.py:212
  57.6 1.9 %collective-permute-done.8 = bf16[128,8,128]{2,1,0:T(8,128)(2,1)S(1)} collective-permute-done((bf16[128,8,128]{2,1,0:T(8,128)(2,1)S(1)}, bf16[128,8,128]{2,1,0:T(8,128)(2,1)S(1)}, u32[]{:S(2)}, u32[]{:S(2)}) %collective-permute-start.8) | collective-permute-done | bytes 262176 | tf_op jit(solution)/shard_map/ppermute | solution.py:278
  59.6 3.0 %collective-permute-done.7 = bf16[128,8,128]{2,1,0:T(8,128)(2,1)S(1)} collective-permute-done((bf16[128,8,128]{2,1,0:T(8,128)(2,1)S(1)}, bf16[128,8,128]{2,1,0:T(8,128)(2,1)S(1)}, u32[]{:S(2)}, u32[]{:S(2)}) %collective-permute-start.7) | collective-permute-done | bytes 262176 | tf_op jit(solution)/shard_map/ppermute | solution.py:278
  62.6 0.1 pad_maximum_fusion
  62.7 2.4 %collective-permute-start.11 = (bf16[4,128,8,128]{3,2,1,0:T(8,128)(2,1)S(1)}, bf16[4,128,8,128]{3,2,1,0:T(8,128)(2,1)S(1)}, u32[]{:S(2)}, u32[]{:S(2)}) collective-permute-start(bf16[4,128,8,128]{3,2,1,0:T(8,128)(2,1)S(1)} %pad_maximum_fusion), channel_id=1, source_target_pairs={{0,6},{1,7},{2,0},{3,1},{4,2},{5,3},{6,4},{7,5},{8,14},{9,15},{10,... | collective-permute-start | bytes 3145736 | tf_op jit(solution)/shard_map/ppermute | solution.py:278
  65.1 9.3 %shard_map.51 = (f32[128,768]{1,0:T(8,128)S(1)}, bf16[128,768]{1,0:T(8,128)(2,1)S(1)}) custom-call(s32[2]{0:T(128)S(1)} %pad_add_fusion.1.place_ref, f32[32,8,3,32,128]{4,3,2,1,0:T(8,128)S(1)} %shard_map.49.r_ref, bf16[8192,768]{1,0:T(8,128)(2,1)S(1)} %shard_map.48.t_ref, bf16[512,8,128]{2,1,0:T(8,128)(2,1)S(1)} %bitcast.40, f32[256,768]{1,0:T(8,128)S(1)} %shard_map.50.refs_1_), custom_call_target="tpu_custom_call" | custom-call | flops 7247757312 | bytes 12582912 | tf_op jit(solution)/shard_map/pallas_call | solution.py:212
  74.5 1.1 collective-permute-start.13
  75.6 1.3 %collective-permute-done.11 = bf16[4,128,8,128]{3,2,1,0:T(8,128)(2,1)S(1)} collective-permute-done((bf16[4,128,8,128]{3,2,1,0:T(8,128)(2,1)S(1)}, bf16[4,128,8,128]{3,2,1,0:T(8,128)(2,1)S(1)}, u32[]{:S(2)}, u32[]{:S(2)}) %collective-permute-start.11) | collective-permute-done | bytes 1048608 | tf_op jit(solution)/shard_map/ppermute | solution.py:278
  76.9 3.4 %collective-permute-done.10 = bf16[4,128,8,128]{3,2,1,0:T(8,128)(2,1)S(1)} collective-permute-done((bf16[4,128,8,128]{3,2,1,0:T(8,128)(2,1)S(1)}, bf16[4,128,8,128]{3,2,1,0:T(8,128)(2,1)S(1)}, u32[]{:S(2)}, u32[]{:S(2)}) %collective-permute-start.10) | collective-permute-done | bytes 1048608 | tf_op jit(solution)/shard_map/ppermute | solution.py:278
  80.3 23.0 %shard_map.52 = (f32[256,768]{1,0:T(8,128)S(1)}, bf16[256,768]{1,0:T(8,128)(2,1)S(1)}) custom-call(s32[2]{0:T(128)S(1)} %pad_add_fusion.1.place_ref, f32[32,8,3,32,128]{4,3,2,1,0:T(8,128)S(1)} %shard_map.49.r_ref, bf16[8192,768]{1,0:T(8,128)(2,1)S(1)} %shard_map.48.t_ref, bf16[512,8,128]{2,1,0:T(8,128)(2,1)S(1)} %bitcast.47, bf16[512,8,128]{2,1,0:T(8,128)(2,1)S(1)} %bitcast.46), custom_call_target="tpu_custom_call" | custom-call | flops 19327352832 | bytes 12582912 | tf_op jit(solution)/shard_map/pallas_call | solution.py:212
  103.3 1.1 collective-permute-start.14
  104.4 7.1 %shard_map.53 = bf16[128,768]{1,0:T(8,128)(2,1)S(1)} custom-call(s32[2]{0:T(128)S(1)} %pad_add_fusion.1.place_ref, f32[32,8,3,32,128]{4,3,2,1,0:T(8,128)S(1)} %shard_map.49.r_ref, bf16[8192,768]{1,0:T(8,128)(2,1)S(1)} %shard_map.48.t_ref, bf16[512,8,128]{2,1,0:T(8,128)(2,1)S(1)} %bitcast.38), custom_call_target="tpu_custom_call" | custom-call | flops 4831838208 | bytes 12582912 | tf_op jit(solution)/shard_map/pallas_call | solution.py:212
  111.4 0.5 collective-permute-start.15
  112.0 7.1 %shard_map.54.refs_2_ = f32[128,768]{1,0:T(8,128)S(1)} custom-call(s32[2]{0:T(128)S(1)} %pad_add_fusion.1.place_ref, f32[32,8,3,32,128]{4,3,2,1,0:T(8,128)S(1)} %shard_map.49.r_ref, bf16[8192,768]{1,0:T(8,128)(2,1)S(1)} %shard_map.48.t_ref, bf16[512,8,128]{2,1,0:T(8,128)(2,1)S(1)} %bitcast.39), custom_call_target="tpu_custom_call" | custom-call | flops 4831838208 | bytes 12582912 | tf_op jit(solution)/shard_map/pallas_call | solution.py:212
  119.1 0.7 shard_map.55
  119.8 6.5 %collective-permute-start.16 = (bf16[4,64,768]{2,1,0:T(8,128)(2,1)S(1)}, bf16[4,64,768]{2,1,0:T(8,128)(2,1)S(1)}, u32[]{:S(2)}, u32[]{:S(2)}) collective-permute-start(bf16[4,64,768]{2,1,0:T(8,128)(2,1)S(1)} %get-tuple-element.88), channel_id=1, source_target_pairs={{0,32},{32,0},{64,96},{96,64},{1,33},{33,1},{65,97},{97,65},{2,34}... | collective-permute-start | bytes 1179656 | tf_op jit(solution)/shard_map/ppermute | solution.py:359
  126.3 1.3 %collective-permute-done.16 = bf16[4,64,768]{2,1,0:T(8,128)(2,1)S(1)} collective-permute-done((bf16[4,64,768]{2,1,0:T(8,128)(2,1)S(1)}, bf16[4,64,768]{2,1,0:T(8,128)(2,1)S(1)}, u32[]{:S(2)}, u32[]{:S(2)}) %collective-permute-start.16) | collective-permute-done | bytes 393248 | tf_op jit(solution)/shard_map/ppermute | solution.py:359
  127.7 0.1 convert_add_fusion
  127.8 0.9 copy.5
  (14 shorter events, 0.1 us)
Async XLA Ops:
  1.6 2.2 %copy-start = (bf16[8,2,32,4096]{3,2,1,0:T(8,128)(2,1)S(1)}, bf16[8,2,32,4096]{3,2,1,0:T(8,128)(2,1)}, u32[]{:S(2)}) copy-start(bf16[8,2,32,4096]{3,2,1,0:T(8,128)(2,1)} %s_ref.3) | copy-start | bytes 12582916
  3.8 6.2 %copy-start.1 = (bf16[8,2,32,4096]{3,2,1,0:T(8,128)(2,1)S(1)}, bf16[8,2,32,4096]{3,2,1,0:T(8,128)(2,1)}, u32[]{:S(2)}) copy-start(bf16[8,2,32,4096]{3,2,1,0:T(8,128)(2,1)} %r_ref.1) | copy-start | bytes 12582916
  4.4 16.2 %collective-permute-start.1 = (bf16[4,128,8,128]{3,2,1,0:T(8,128)(2,1)S(1)}, bf16[4,128,8,128]{3,2,1,0:T(8,128)(2,1)S(1)}, u32[]{:S(2)}, u32[]{:S(2)}) collective-permute-start(bf16[4,128,8,128]{3,2,1,0:T(8,128)(2,1)S(1)} %bitcast.45), channel_id=1, source_target_pairs={{0,4},{1,5},{2,6},{3,7},{4,0},{5,1},{6,2},{7,3},{8,12},{9,13},{10,... | collective-permute-start | bytes 3145736 | tf_op jit(solution)/shard_map/ppermute | solution.py:278
  8.0 24.1 %collective-permute-start = (bf16[4,128,8,128]{3,2,1,0:T(8,128)(2,1)S(1)}, bf16[4,128,8,128]{3,2,1,0:T(8,128)(2,1)S(1)}, u32[]{:S(2)}, u32[]{:S(2)}) collective-permute-start(bf16[4,128,8,128]{3,2,1,0:T(8,128)(2,1)S(1)} %bitcast.44), channel_id=1, source_target_pairs={{0,6},{1,7},{2,0},{3,1},{4,2},{5,3},{6,4},{7,5},{8,14},{9,15},{10,... | collective-permute-start | bytes 3145736 | tf_op jit(solution)/shard_map/ppermute | solution.py:278
  8.9 23.2 %collective-permute-start.2 = (bf16[4,128,8,128]{3,2,1,0:T(8,128)(2,1)S(1)}, bf16[4,128,8,128]{3,2,1,0:T(8,128)(2,1)S(1)}, u32[]{:S(2)}, u32[]{:S(2)}) collective-permute-start(bf16[4,128,8,128]{3,2,1,0:T(8,128)(2,1)S(1)} %bitcast.43), channel_id=1, source_target_pairs={{0,2},{1,3},{2,4},{3,5},{4,6},{5,7},{6,0},{7,1},{8,10},{9,11},{10,... | collective-permute-start | bytes 3145736 | tf_op jit(solution)/shard_map/ppermute | solution.py:278
  32.4 6.9 %collective-permute-start.5 = (bf16[128,8,128]{2,1,0:T(8,128)(2,1)S(1)}, bf16[128,8,128]{2,1,0:T(8,128)(2,1)S(1)}, u32[]{:S(2)}, u32[]{:S(2)}) collective-permute-start(bf16[128,8,128]{2,1,0:T(8,128)(2,1)S(1)} %get-tuple-element.89), channel_id=1, source_target_pairs={{0,8},{1,9},{2,10},{3,11},{4,12},{5,13},{6,14},{7,15},{8,16},{9,17... | collective-permute-start | bytes 786440 | tf_op jit(solution)/shard_map/ppermute | solution.py:278
  34.6 8.6 %collective-permute-start.4 = (bf16[128,8,128]{2,1,0:T(8,128)(2,1)S(1)}, bf16[128,8,128]{2,1,0:T(8,128)(2,1)S(1)}, u32[]{:S(2)}, u32[]{:S(2)}) collective-permute-start(bf16[128,8,128]{2,1,0:T(8,128)(2,1)S(1)} %get-tuple-element.90), channel_id=1, source_target_pairs={{0,16},{1,17},{2,18},{3,19},{4,20},{5,21},{6,22},{7,23},{8,24},{9,... | collective-permute-start | bytes 786440 | tf_op jit(solution)/shard_map/ppermute | solution.py:278
  36.4 6.9 %collective-permute-start.3 = (bf16[128,8,128]{2,1,0:T(8,128)(2,1)S(1)}, bf16[128,8,128]{2,1,0:T(8,128)(2,1)S(1)}, u32[]{:S(2)}, u32[]{:S(2)}) collective-permute-start(bf16[128,8,128]{2,1,0:T(8,128)(2,1)S(1)} %get-tuple-element.91), channel_id=1, source_target_pairs={{0,24},{1,25},{2,26},{3,27},{4,28},{5,29},{6,30},{7,31},{8,0},{9,1... | collective-permute-start | bytes 786440 | tf_op jit(solution)/shard_map/ppermute | solution.py:278
  43.3 7.9 %collective-permute-start.6 = (bf16[128,8,128]{2,1,0:T(8,128)(2,1)S(1)}, bf16[128,8,128]{2,1,0:T(8,128)(2,1)S(1)}, u32[]{:S(2)}, u32[]{:S(2)}) collective-permute-start(bf16[128,8,128]{2,1,0:T(8,128)(2,1)S(1)} %fusion.1), channel_id=1, source_target_pairs={{0,1},{1,0},{2,3},{3,2},{4,5},{5,4},{6,7},{7,6},{8,9},{9,8},{10,11... | collective-permute-start | bytes 786440 | tf_op jit(solution)/shard_map/ppermute | solution.py:281
  51.3 6.3 %collective-permute-start.9 = (bf16[128,8,128]{2,1,0:T(8,128)(2,1)S(1)}, bf16[128,8,128]{2,1,0:T(8,128)(2,1)S(1)}, u32[]{:S(2)}, u32[]{:S(2)}) collective-permute-start(bf16[128,8,128]{2,1,0:T(8,128)(2,1)S(1)} %broadcast_select_fusion.refs_0_), channel_id=1, source_target_pairs={{0,24},{1,25},{2,26},{3,27},{4,28},{5,29},{6,30},{7,31},{8,0},{9,1... | collective-permute-start | bytes 786440 | tf_op jit(solution)/shard_map/ppermute | solution.py:278
  52.7 6.8 %collective-permute-start.8 = (bf16[128,8,128]{2,1,0:T(8,128)(2,1)S(1)}, bf16[128,8,128]{2,1,0:T(8,128)(2,1)S(1)}, u32[]{:S(2)}, u32[]{:S(2)}) collective-permute-start(bf16[128,8,128]{2,1,0:T(8,128)(2,1)S(1)} %broadcast_select_fusion.refs_0_), channel_id=1, source_target_pairs={{0,16},{1,17},{2,18},{3,19},{4,20},{5,21},{6,22},{7,23},{8,24},{9,... | collective-permute-start | bytes 786440 | tf_op jit(solution)/shard_map/ppermute | solution.py:278
  54.0 8.6 %collective-permute-start.7 = (bf16[128,8,128]{2,1,0:T(8,128)(2,1)S(1)}, bf16[128,8,128]{2,1,0:T(8,128)(2,1)S(1)}, u32[]{:S(2)}, u32[]{:S(2)}) collective-permute-start(bf16[128,8,128]{2,1,0:T(8,128)(2,1)S(1)} %broadcast_select_fusion.refs_0_), channel_id=1, source_target_pairs={{0,8},{1,9},{2,10},{3,11},{4,12},{5,13},{6,14},{7,15},{8,16},{9,17... | collective-permute-start | bytes 786440 | tf_op jit(solution)/shard_map/ppermute | solution.py:278
  62.7 14.2 %collective-permute-start.11 = (bf16[4,128,8,128]{3,2,1,0:T(8,128)(2,1)S(1)}, bf16[4,128,8,128]{3,2,1,0:T(8,128)(2,1)S(1)}, u32[]{:S(2)}, u32[]{:S(2)}) collective-permute-start(bf16[4,128,8,128]{3,2,1,0:T(8,128)(2,1)S(1)} %pad_maximum_fusion), channel_id=1, source_target_pairs={{0,6},{1,7},{2,0},{3,1},{4,2},{5,3},{6,4},{7,5},{8,14},{9,15},{10,... | collective-permute-start | bytes 3145736 | tf_op jit(solution)/shard_map/ppermute | solution.py:278
  65.1 15.2 %collective-permute-start.10 = (bf16[4,128,8,128]{3,2,1,0:T(8,128)(2,1)S(1)}, bf16[4,128,8,128]{3,2,1,0:T(8,128)(2,1)S(1)}, u32[]{:S(2)}, u32[]{:S(2)}) collective-permute-start(bf16[4,128,8,128]{3,2,1,0:T(8,128)(2,1)S(1)} %pad_maximum_fusion), channel_id=1, source_target_pairs={{0,2},{1,3},{2,4},{3,5},{4,6},{5,7},{6,0},{7,1},{8,10},{9,11},{10,... | collective-permute-start | bytes 3145736 | tf_op jit(solution)/shard_map/ppermute | solution.py:278
  74.5 44.6 %collective-permute-start.13 = (bf16[128,768]{1,0:T(8,128)(2,1)S(1)}, bf16[128,768]{1,0:T(8,128)(2,1)S(1)}, u32[]{:S(2)}, u32[]{:S(2)}) collective-permute-start(bf16[128,768]{1,0:T(8,128)(2,1)S(1)} %get-tuple-element.84), channel_id=1, source_target_pairs={{0,64},{64,0},{32,96},{96,32},{1,65},{65,1},{33,97},{97,33},{2,66}... | collective-permute-start | bytes 589832 | tf_op jit(solution)/shard_map/ppermute | solution.py:357
  80.3 24.1 %collective-permute-start.12 = (bf16[4,128,8,128]{3,2,1,0:T(8,128)(2,1)S(1)}, bf16[4,128,8,128]{3,2,1,0:T(8,128)(2,1)S(1)}, u32[]{:S(2)}, u32[]{:S(2)}) collective-permute-start(bf16[4,128,8,128]{3,2,1,0:T(8,128)(2,1)S(1)} %pad_maximum_fusion), channel_id=1, source_target_pairs={{0,4},{1,5},{2,6},{3,7},{4,0},{5,1},{6,2},{7,3},{8,12},{9,13},{10,... | collective-permute-start | bytes 3145736 | tf_op jit(solution)/shard_map/ppermute | solution.py:278
  103.3 15.8 %collective-permute-start.14 = (bf16[256,768]{1,0:T(8,128)(2,1)S(1)}, bf16[256,768]{1,0:T(8,128)(2,1)S(1)}, u32[]{:S(2)}, u32[]{:S(2)}) collective-permute-start(bf16[256,768]{1,0:T(8,128)(2,1)S(1)} %get-tuple-element.85), channel_id=1, source_target_pairs={{0,64},{64,0},{32,96},{96,32},{1,65},{65,1},{33,97},{97,33},{2,66}... | collective-permute-start | bytes 1179656 | tf_op jit(solution)/shard_map/ppermute | solution.py:357
  111.4 7.6 %collective-permute-start.15 = (bf16[128,768]{1,0:T(8,128)(2,1)S(1)}, bf16[128,768]{1,0:T(8,128)(2,1)S(1)}, u32[]{:S(2)}, u32[]{:S(2)}) collective-permute-start(bf16[128,768]{1,0:T(8,128)(2,1)S(1)} %shard_map.53), channel_id=1, source_target_pairs={{0,64},{64,0},{32,96},{96,32},{1,65},{65,1},{33,97},{97,33},{2,66}... | collective-permute-start | bytes 589832 | tf_op jit(solution)/shard_map/ppermute | solution.py:357
  119.8 7.9 %collective-permute-start.16 = (bf16[4,64,768]{2,1,0:T(8,128)(2,1)S(1)}, bf16[4,64,768]{2,1,0:T(8,128)(2,1)S(1)}, u32[]{:S(2)}, u32[]{:S(2)}) collective-permute-start(bf16[4,64,768]{2,1,0:T(8,128)(2,1)S(1)} %get-tuple-element.88), channel_id=1, source_target_pairs={{0,32},{32,0},{64,96},{96,64},{1,33},{33,1},{65,97},{97,65},{2,34}... | collective-permute-start | bytes 1179656 | tf_op jit(solution)/shard_map/ppermute | solution.py:359

commit v4 on v3

--- a/solution.py
+++ b/solution.py
@@ -119,7 +119,7 @@
     )(spectra, flags)
 
 
-def lag_quarters(receiving, tiles, table, place, side=None, nears=None, before=None):
+def lag_quarters(receiving, tiles, table, place, side=None, nears=None, before=None, held=0):
     columns, windows, _, receivers, _ = receiving.shape
     parts = 2
     bins = columns * LANES
@@ -155,7 +155,7 @@
                 turn = i // wide
                 quarter = lax.rem(place_ref[0] + QUARTERS - nears[0] - turn, QUARTERS)
                 column = quarter * wide + lax.rem(i, wide)
-                base = (nears[0] + turn) * piece + lax.rem(i, wide)
+                base = (nears[0] - held + turn) * piece + lax.rem(i, wide)
                 real_column = turn * 2 * wide + lax.rem(i, wide)
                 imag_column = real_column + wide
             to_real = pl.ds(pl.multiple_of(real_column * LANES, LANES), LANES)
@@ -334,18 +334,27 @@
     mine = jnp.where(same_z, mine, grid.flip(mine))
     near = [mine] + [grid.move(mine, 0, d) for d in steps]
     (early,) = lag_quarters(receiving, [mine], table, lag_place, nears=(0,))
+    first = jnp.stack(near[:2])
+    first_halves = {d: grid.move(first, 1, d) for d in (1, 3)}
     near, early = lax.optimization_barrier((near, early))
     row = jnp.stack(near)
-    quarters = [row, grid.move(row, 1, 1), None, grid.move(row, 1, 3)]
+    second = jnp.stack(near[2:])
+    quarters = [row, grid.move(second, 1, 1), None, grid.move(second, 1, 3)]
 
     kept, received = [], []
     for group in GROUPS:
         if group == GROUPS[1]:
-            row, quarters[1], quarters[3] = lax.optimization_barrier((row, quarters[1], quarters[3]))
+            blocks = [first_halves[d].reshape(tiles // 2, ROWS, LANES) for d in group]
+            (half,) = lag_quarters(receiving, blocks, table, lag_place, nears=(0, 1))
+            row, quarters[1], quarters[3], half = lax.optimization_barrier((row, quarters[1], quarters[3], half))
             quarters[2] = grid.move(row, 1, 2)
-        blocks = [quarters[d].reshape(tiles, ROWS, LANES) for d in group]
+            blocks = [quarters[d].reshape(tiles // 2, ROWS, LANES) for d in group]
+        else:
+            blocks = [quarters[d].reshape(tiles, ROWS, LANES) for d in group]
         if group == GROUPS[0]:
             mine, given = lag_quarters(receiving, blocks, table, lag_place, nears=(1, 2, 3), before=early)
+        elif group == GROUPS[1]:
+            mine, given = lag_quarters(receiving, blocks, table, lag_place, nears=(2, 3), before=half, held=2)
         elif group != GROUPS[-1]:
             mine, given = lag_quarters(receiving, blocks, table, lag_place)
         else:

time: 129 us -> 129 us (level); the launches traced: 129 us -> 127 us
  waiting for transfers between devices: 35.8 us -> 28.3 us
  starting transfers between devices: 28.3 us -> 33.3 us
    ppermute x12 -> x14, waiting for transfers between devices: 30.3 us -> 22.1 us  [move(): return lax.ppermute(value, ('win', 'rcv'), self.pairs[axis, step])]
    ppermute x12 -> x14, starting transfers between devices: 15.4 us -> 18.1 us  [move(): return lax.ppermute(value, ('win', 'rcv'), self.pairs[axis, step])]
    ppermute x1, starting transfers between devices: 6.54 us -> 8.18 us  [local(): lax.ppermute(given, 'win', [(0, 1), (1, 0), (2, 3), (3, 2)])]
    pallas_call x5 -> x6, Pallas kernels: 50 us -> 50.8 us  [lag_quarters(): pl.pallas_call(kernel, in_specs=[pl.BlockSpec(memory_space=pltpu.SMEM)] +...]
  transfers between devices with their start and end apart: 17 -> 19, of which waited for: 10 -> 9; matrix products, arithmetic and copies ran while one was open for 1% -> 1% of each run, Pallas kernels for 44% -> 45%
where the time goes in v4:
time: 129 us; the launch traced here: 127 us
  Pallas kernels  58.2 us (45%)
  starting transfers between devices  33.3 us (26%)
  waiting for transfers between devices  28.3 us (22%)
  local copies, waits for them, and re-layouts  3.27 us (3%)
  other arithmetic  3.08 us (2%)
    pallas_call x6, Pallas kernels, lag_quarters(): pl.pallas_call(kernel, in_specs=[pl.BlockSpec(memory_space=pltpu.SMEM)] +...  50.8 us
    ppermute x14, waiting for transfers between devices, move(): return lax.ppermute(value, ('win', 'rcv'), self.pairs[axis, step])  22.1 us
    ppermute x14, starting transfers between devices, move(): return lax.ppermute(value, ('win', 'rcv'), self.pairs[axis, step])  18.1 us
    ppermute x1, starting transfers between devices, local(): lax.ppermute(given, 'win', [(0, 1), (1, 0), (2, 3), (3, 2)])  8.18 us
    ppermute x1, waiting for transfers between devices, flip(): return lax.ppermute(value, 'rcv', [(i, i ^ 1) for i in range(32)])  4.9 us
    ppermute x1, starting transfers between devices, flip(): return lax.ppermute(value, 'rcv', [(i, i ^ 1) for i in range(32)])  4.68 us
    pallas_call x1, Pallas kernels, build_table(): pl.pallas_call(kernel, in_specs=[in_vmem] * 4, out_specs=in_vmem, out_sha...  4.21 us
  transfers between devices with their start and end apart: 19, of which 9 were waited for; matrix products, arithmetic and copies ran while one was open for 1% of the time, Pallas kernels for 45%

profile of v4, /device:TPU:1, one launch (start us, length us, event | category | flops | bytes accessed | tf_op | source)
XLA Modules:
  0.0 127.1 jit_solution(3091297805949811592)
XLA Ops:
  0.7 0.1 pad_add_fusion.1.place_ref
  0.8 0.7 convert_element_type.33
  1.5 0.1 broadcast_in_dim.2.f_ref
  1.6 2.2 %copy-done = bf16[8,2,32,4096]{3,2,1,0:T(8,128)(2,1)S(1)} copy-done((bf16[8,2,32,4096]{3,2,1,0:T(8,128)(2,1)S(1)}, bf16[8,2,32,4096]{3,2,1,0:T(8,128)(2,1)}, u32[]{:S(2)}) %copy-start) | copy-done | bytes 4194328
  3.8 0.5 shard_map.46
  4.4 3.7 %collective-permute-start.1 = (bf16[4,128,8,128]{3,2,1,0:T(8,128)(2,1)S(1)}, bf16[4,128,8,128]{3,2,1,0:T(8,128)(2,1)S(1)}, u32[]{:S(2)}, u32[]{:S(2)}) collective-permute-start(bf16[4,128,8,128]{3,2,1,0:T(8,128)(2,1)S(1)} %bitcast.50), channel_id=1, source_target_pairs={{0,4},{1,5},{2,6},{3,7},{4,0},{5,1},{6,2},{7,3},{8,12},{9,13},{10,... | collective-permute-start | bytes 3145736 | tf_op jit(solution)/shard_map/ppermute | solution.py:278
  8.0 0.9 collective-permute-start
  8.9 0.6 collective-permute-start.2
  9.5 0.5 shard_map.47
  10.1 1.4 %shard_map.49.r_ref = f32[32,8,3,32,128]{4,3,2,1,0:T(8,128)S(1)} custom-call(bf16[8,2,32,4096]{3,2,1,0:T(8,128)(2,1)S(1)} %copy-done.1, f32[8,32,128]{2,1,0:T(8,128)S(1)} %broadcast_in_dim.2.f_ref), custom_call_target="tpu_custom_call" | custom-call | flops 8388608 | bytes 16777216 | tf_op jit(solution)/shard_map/pallas_call | solution.py:112
  11.5 1.6 %fusion.11 = (f32[64,768]{1,0:T(8,128)S(1)}, f32[64,768]{1,0:T(8,128)S(1)}, f32[64,768]{1,0:T(8,128)S(1)}, f32[64,768]{1,0:T(8,128)S(1)}) fusion(s32[768]{0:T(1024)S(1)} %iota_add_fusion, s32[64]{0:T(128)S(1)} %iota_multiply_fusion), kind=kLoop, calls=%fused_computation.31 | loop fusion | flops 1474560 | bytes 789760 | tf_op jit(solution)/shard_map/sin | solution.py:30
  13.1 4.2 %shard_map.48.t_ref = bf16[8192,768]{1,0:T(8,128)(2,1)S(1)} custom-call(f32[64,768]{1,0:T(8,128)S(1)} %get-tuple-element.97.cos_low, f32[64,768]{1,0:T(8,128)S(1)} %get-tuple-element.96.sin_low, f32[64,768]{1,0:T(8,128)S(1)} %get-tuple-element.95.cos_high, f32[64,768]{1,0:T(8,128)S(1)} %get-tuple-element.94.sin_high), custom_call_target="tpu_custom_call" | custom-call | flops 50331648 | bytes 12582912 | tf_op jit(solution)/shard_map/pallas_call | solution.py:47
  17.3 3.2 %collective-permute-done.1 = bf16[4,128,8,128]{3,2,1,0:T(8,128)(2,1)S(1)} collective-permute-done((bf16[4,128,8,128]{3,2,1,0:T(8,128)(2,1)S(1)}, bf16[4,128,8,128]{3,2,1,0:T(8,128)(2,1)S(1)}, u32[]{:S(2)}, u32[]{:S(2)}) %collective-permute-start.1) | collective-permute-done | bytes 1048608 | tf_op jit(solution)/shard_map/ppermute | solution.py:278
  20.6 11.5 %collective-permute-done = bf16[4,128,8,128]{3,2,1,0:T(8,128)(2,1)S(1)} collective-permute-done((bf16[4,128,8,128]{3,2,1,0:T(8,128)(2,1)S(1)}, bf16[4,128,8,128]{3,2,1,0:T(8,128)(2,1)S(1)}, u32[]{:S(2)}, u32[]{:S(2)}) %collective-permute-start) | collective-permute-done | bytes 1048608 | tf_op jit(solution)/shard_map/ppermute | solution.py:278
  32.1 0.2 select_select_fusion
  32.4 1.4 %collective-permute-start.5 = (bf16[128,8,128]{2,1,0:T(8,128)(2,1)S(1)}, bf16[128,8,128]{2,1,0:T(8,128)(2,1)S(1)}, u32[]{:S(2)}, u32[]{:S(2)}) collective-permute-start(bf16[128,8,128]{2,1,0:T(8,128)(2,1)S(1)} %get-tuple-element.91), channel_id=1, source_target_pairs={{0,8},{1,9},{2,10},{3,11},{4,12},{5,13},{6,14},{7,15},{8,16},{9,17... | collective-permute-start | bytes 786440 | tf_op jit(solution)/shard_map/ppermute | solution.py:278
  33.8 2.6 %collective-permute-start.4 = (bf16[128,8,128]{2,1,0:T(8,128)(2,1)S(1)}, bf16[128,8,128]{2,1,0:T(8,128)(2,1)S(1)}, u32[]{:S(2)}, u32[]{:S(2)}) collective-permute-start(bf16[128,8,128]{2,1,0:T(8,128)(2,1)S(1)} %get-tuple-element.92), channel_id=1, source_target_pairs={{0,16},{1,17},{2,18},{3,19},{4,20},{5,21},{6,22},{7,23},{8,24},{9,... | collective-permute-start | bytes 786440 | tf_op jit(solution)/shard_map/ppermute | solution.py:278
  36.4 1.1 collective-permute-start.3
  37.5 1.8 %collective-permute-done.5 = bf16[128,8,128]{2,1,0:T(8,128)(2,1)S(1)} collective-permute-done((bf16[128,8,128]{2,1,0:T(8,128)(2,1)S(1)}, bf16[128,8,128]{2,1,0:T(8,128)(2,1)S(1)}, u32[]{:S(2)}, u32[]{:S(2)}) %collective-permute-start.5) | collective-permute-done | bytes 262176 | tf_op jit(solution)/shard_map/ppermute | solution.py:278
  39.3 4.0 %collective-permute-done.4 = bf16[128,8,128]{2,1,0:T(8,128)(2,1)S(1)} collective-permute-done((bf16[128,8,128]{2,1,0:T(8,128)(2,1)S(1)}, bf16[128,8,128]{2,1,0:T(8,128)(2,1)S(1)}, u32[]{:S(2)}, u32[]{:S(2)}) %collective-permute-start.4) | collective-permute-done | bytes 262176 | tf_op jit(solution)/shard_map/ppermute | solution.py:278
  43.2 0.1 fusion.1
  43.3 4.7 %collective-permute-start.6 = (bf16[128,8,128]{2,1,0:T(8,128)(2,1)S(1)}, bf16[128,8,128]{2,1,0:T(8,128)(2,1)S(1)}, u32[]{:S(2)}, u32[]{:S(2)}) collective-permute-start(bf16[128,8,128]{2,1,0:T(8,128)(2,1)S(1)} %fusion.1), channel_id=1, source_target_pairs={{0,1},{1,0},{2,3},{3,2},{4,5},{5,4},{6,7},{7,6},{8,9},{9,8},{10,11... | collective-permute-start | bytes 786440 | tf_op jit(solution)/shard_map/ppermute | solution.py:281
  48.0 4.9 %collective-permute-done.6 = bf16[128,8,128]{2,1,0:T(8,128)(2,1)S(1)} collective-permute-done((bf16[128,8,128]{2,1,0:T(8,128)(2,1)S(1)}, bf16[128,8,128]{2,1,0:T(8,128)(2,1)S(1)}, u32[]{:S(2)}, u32[]{:S(2)}) %collective-permute-start.6) | collective-permute-done | bytes 262176 | tf_op jit(solution)/shard_map/ppermute | solution.py:281
  52.9 0.6 collective-permute-start.7
  53.6 2.1 %collective-permute-start.9 = (bf16[128,8,128]{2,1,0:T(8,128)(2,1)S(1)}, bf16[128,8,128]{2,1,0:T(8,128)(2,1)S(1)}, u32[]{:S(2)}, u32[]{:S(2)}) collective-permute-start(bf16[128,8,128]{2,1,0:T(8,128)(2,1)S(1)} %broadcast_select_fusion.refs_0_), channel_id=1, source_target_pairs={{0,24},{1,25},{2,26},{3,27},{4,28},{5,29},{6,30},{7,31},{8,0},{9,1... | collective-permute-start | bytes 786440 | tf_op jit(solution)/shard_map/ppermute | solution.py:278
  55.7 0.1 collective-permute-start.8
  55.8 3.6 %shard_map.50.refs_1_ = f32[256,768]{1,0:T(8,128)S(1)} custom-call(s32[2]{0:T(128)S(1)} %pad_add_fusion.1.place_ref, f32[32,8,3,32,128]{4,3,2,1,0:T(8,128)S(1)} %shard_map.49.r_ref, bf16[8192,768]{1,0:T(8,128)(2,1)S(1)} %shard_map.48.t_ref, bf16[128,8,128]{2,1,0:T(8,128)(2,1)S(1)} %broadcast_select_fusion.refs_0_), custom_call_target="tpu_custom_call" | custom-call | flops 2415919104 | bytes 12582912 | tf_op jit(solution)/shard_map/pallas_call | solution.py:212
  59.5 0.9 collective-permute-start.13
  60.4 0.6 collective-permute-start.12
  61.0 0.8 collective-permute-done.9
  61.8 0.6 collective-permute-done.8
  62.5 0.7 collective-permute-start.11
  63.2 0.8 collective-permute-start.10
  64.0 0.1 pad_maximum_fusion
  64.1 9.3 %shard_map.51 = (f32[128,768]{1,0:T(8,128)S(1)}, bf16[128,768]{1,0:T(8,128)(2,1)S(1)}) custom-call(s32[2]{0:T(128)S(1)} %pad_add_fusion.1.place_ref, f32[32,8,3,32,128]{4,3,2,1,0:T(8,128)S(1)} %shard_map.49.r_ref, bf16[8192,768]{1,0:T(8,128)(2,1)S(1)} %shard_map.48.t_ref, bf16[512,8,128]{2,1,0:T(8,128)(2,1)S(1)} %bitcast.46, f32[256,768]{1,0:T(8,128)S(1)} %shard_map.50.refs_1_), custom_call_target="tpu_custom_call" | custom-call | flops 7247757312 | bytes 12582912 | tf_op jit(solution)/shard_map/pallas_call | solution.py:212
  73.5 11.9 %shard_map.52.refs_2_ = f32[512,768]{1,0:T(8,128)S(1)} custom-call(s32[2]{0:T(128)S(1)} %pad_add_fusion.1.place_ref, f32[32,8,3,32,128]{4,3,2,1,0:T(8,128)S(1)} %shard_map.49.r_ref, bf16[8192,768]{1,0:T(8,128)(2,1)S(1)} %shard_map.48.t_ref, bf16[256,8,128]{2,1,0:T(8,128)(2,1)S(1)} %bitcast.54, bf16[256,8,128]{2,1,0:T(8,128)(2,1)S(1)} %bitcast.53), custom_call_target="tpu_custom_call" | custom-call | flops 9663676416 | bytes 12582912 | tf_op jit(solution)/shard_map/pallas_call | solution.py:212
  85.4 2.0 %collective-permute-start.14 = (bf16[4,128,8,128]{3,2,1,0:T(8,128)(2,1)S(1)}, bf16[4,128,8,128]{3,2,1,0:T(8,128)(2,1)S(1)}, u32[]{:S(2)}, u32[]{:S(2)}) collective-permute-start(bf16[4,128,8,128]{3,2,1,0:T(8,128)(2,1)S(1)} %pad_maximum_fusion), channel_id=1, source_target_pairs={{0,4},{1,5},{2,6},{3,7},{4,0},{5,1},{6,2},{7,3},{8,12},{9,13},{10,... | collective-permute-start | bytes 3145736 | tf_op jit(solution)/shard_map/ppermute | solution.py:278
  87.4 0.7 collective-permute-start.15
  88.1 11.9 %shard_map.53 = (f32[256,768]{1,0:T(8,128)S(1)}, bf16[256,768]{1,0:T(8,128)(2,1)S(1)}) custom-call(s32[2]{0:T(128)S(1)} %pad_add_fusion.1.place_ref, f32[32,8,3,32,128]{4,3,2,1,0:T(8,128)S(1)} %shard_map.49.r_ref, bf16[8192,768]{1,0:T(8,128)(2,1)S(1)} %shard_map.48.t_ref, bf16[256,8,128]{2,1,0:T(8,128)(2,1)S(1)} %bitcast.52, ...), custom_call_target="tpu_custom_call" | custom-call | flops 9663676416 | bytes 12582912 | tf_op jit(solution)/shard_map/pallas_call | solution.py:212
  100.0 0.8 collective-permute-start.16
  100.9 7.1 %shard_map.54 = bf16[128,768]{1,0:T(8,128)(2,1)S(1)} custom-call(s32[2]{0:T(128)S(1)} %pad_add_fusion.1.place_ref, f32[32,8,3,32,128]{4,3,2,1,0:T(8,128)S(1)} %shard_map.49.r_ref, bf16[8192,768]{1,0:T(8,128)(2,1)S(1)} %shard_map.48.t_ref, bf16[512,8,128]{2,1,0:T(8,128)(2,1)S(1)} %bitcast.44), custom_call_target="tpu_custom_call" | custom-call | flops 4831838208 | bytes 12582912 | tf_op jit(solution)/shard_map/pallas_call | solution.py:212
  108.0 0.7 collective-permute-start.17
  108.7 7.1 %shard_map.55.refs_2_ = f32[128,768]{1,0:T(8,128)S(1)} custom-call(s32[2]{0:T(128)S(1)} %pad_add_fusion.1.place_ref, f32[32,8,3,32,128]{4,3,2,1,0:T(8,128)S(1)} %shard_map.49.r_ref, bf16[8192,768]{1,0:T(8,128)(2,1)S(1)} %shard_map.48.t_ref, bf16[512,8,128]{2,1,0:T(8,128)(2,1)S(1)} %bitcast.45), custom_call_target="tpu_custom_call" | custom-call | flops 4831838208 | bytes 12582912 | tf_op jit(solution)/shard_map/pallas_call | solution.py:212
  115.9 0.7 shard_map.56
  116.5 8.2 %collective-permute-start.18 = (bf16[4,64,768]{2,1,0:T(8,128)(2,1)S(1)}, bf16[4,64,768]{2,1,0:T(8,128)(2,1)S(1)}, u32[]{:S(2)}, u32[]{:S(2)}) collective-permute-start(bf16[4,64,768]{2,1,0:T(8,128)(2,1)S(1)} %get-tuple-element.90), channel_id=1, source_target_pairs={{0,32},{32,0},{64,96},{96,64},{1,33},{33,1},{65,97},{97,65},{2,34}... | collective-permute-start | bytes 1179656 | tf_op jit(solution)/shard_map/ppermute | solution.py:368
  124.7 1.3 %collective-permute-done.18 = bf16[4,64,768]{2,1,0:T(8,128)(2,1)S(1)} collective-permute-done((bf16[4,64,768]{2,1,0:T(8,128)(2,1)S(1)}, bf16[4,64,768]{2,1,0:T(8,128)(2,1)S(1)}, u32[]{:S(2)}, u32[]{:S(2)}) %collective-permute-start.18) | collective-permute-done | bytes 393248 | tf_op jit(solution)/shard_map/ppermute | solution.py:368
  126.1 0.1 convert_add_fusion
  126.2 0.9 copy.5
  (21 shorter events, 0.4 us)
Async XLA Ops:
  1.6 2.2 %copy-start = (bf16[8,2,32,4096]{3,2,1,0:T(8,128)(2,1)S(1)}, bf16[8,2,32,4096]{3,2,1,0:T(8,128)(2,1)}, u32[]{:S(2)}) copy-start(bf16[8,2,32,4096]{3,2,1,0:T(8,128)(2,1)} %s_ref.3) | copy-start | bytes 12582916
  3.8 6.2 %copy-start.1 = (bf16[8,2,32,4096]{3,2,1,0:T(8,128)(2,1)S(1)}, bf16[8,2,32,4096]{3,2,1,0:T(8,128)(2,1)}, u32[]{:S(2)}) copy-start(bf16[8,2,32,4096]{3,2,1,0:T(8,128)(2,1)} %r_ref.1) | copy-start | bytes 12582916
  4.4 16.2 %collective-permute-start.1 = (bf16[4,128,8,128]{3,2,1,0:T(8,128)(2,1)S(1)}, bf16[4,128,8,128]{3,2,1,0:T(8,128)(2,1)S(1)}, u32[]{:S(2)}, u32[]{:S(2)}) collective-permute-start(bf16[4,128,8,128]{3,2,1,0:T(8,128)(2,1)S(1)} %bitcast.50), channel_id=1, source_target_pairs={{0,4},{1,5},{2,6},{3,7},{4,0},{5,1},{6,2},{7,3},{8,12},{9,13},{10,... | collective-permute-start | bytes 3145736 | tf_op jit(solution)/shard_map/ppermute | solution.py:278
  8.0 24.1 %collective-permute-start = (bf16[4,128,8,128]{3,2,1,0:T(8,128)(2,1)S(1)}, bf16[4,128,8,128]{3,2,1,0:T(8,128)(2,1)S(1)}, u32[]{:S(2)}, u32[]{:S(2)}) collective-permute-start(bf16[4,128,8,128]{3,2,1,0:T(8,128)(2,1)S(1)} %bitcast.49), channel_id=1, source_target_pairs={{0,6},{1,7},{2,0},{3,1},{4,2},{5,3},{6,4},{7,5},{8,14},{9,15},{10,... | collective-permute-start | bytes 3145736 | tf_op jit(solution)/shard_map/ppermute | solution.py:278
  8.9 23.2 %collective-permute-start.2 = (bf16[4,128,8,128]{3,2,1,0:T(8,128)(2,1)S(1)}, bf16[4,128,8,128]{3,2,1,0:T(8,128)(2,1)S(1)}, u32[]{:S(2)}, u32[]{:S(2)}) collective-permute-start(bf16[4,128,8,128]{3,2,1,0:T(8,128)(2,1)S(1)} %bitcast.48), channel_id=1, source_target_pairs={{0,2},{1,3},{2,4},{3,5},{4,6},{5,7},{6,0},{7,1},{8,10},{9,11},{10,... | collective-permute-start | bytes 3145736 | tf_op jit(solution)/shard_map/ppermute | solution.py:278
  32.4 6.9 %collective-permute-start.5 = (bf16[128,8,128]{2,1,0:T(8,128)(2,1)S(1)}, bf16[128,8,128]{2,1,0:T(8,128)(2,1)S(1)}, u32[]{:S(2)}, u32[]{:S(2)}) collective-permute-start(bf16[128,8,128]{2,1,0:T(8,128)(2,1)S(1)} %get-tuple-element.91), channel_id=1, source_target_pairs={{0,8},{1,9},{2,10},{3,11},{4,12},{5,13},{6,14},{7,15},{8,16},{9,17... | collective-permute-start | bytes 786440 | tf_op jit(solution)/shard_map/ppermute | solution.py:278
  33.8 9.5 %collective-permute-start.4 = (bf16[128,8,128]{2,1,0:T(8,128)(2,1)S(1)}, bf16[128,8,128]{2,1,0:T(8,128)(2,1)S(1)}, u32[]{:S(2)}, u32[]{:S(2)}) collective-permute-start(bf16[128,8,128]{2,1,0:T(8,128)(2,1)S(1)} %get-tuple-element.92), channel_id=1, source_target_pairs={{0,16},{1,17},{2,18},{3,19},{4,20},{5,21},{6,22},{7,23},{8,24},{9,... | collective-permute-start | bytes 786440 | tf_op jit(solution)/shard_map/ppermute | solution.py:278
  36.4 6.9 %collective-permute-start.3 = (bf16[128,8,128]{2,1,0:T(8,128)(2,1)S(1)}, bf16[128,8,128]{2,1,0:T(8,128)(2,1)S(1)}, u32[]{:S(2)}, u32[]{:S(2)}) collective-permute-start(bf16[128,8,128]{2,1,0:T(8,128)(2,1)S(1)} %get-tuple-element.93), channel_id=1, source_target_pairs={{0,24},{1,25},{2,26},{3,27},{4,28},{5,29},{6,30},{7,31},{8,0},{9,1... | collective-permute-start | bytes 786440 | tf_op jit(solution)/shard_map/ppermute | solution.py:278
  43.3 9.6 %collective-permute-start.6 = (bf16[128,8,128]{2,1,0:T(8,128)(2,1)S(1)}, bf16[128,8,128]{2,1,0:T(8,128)(2,1)S(1)}, u32[]{:S(2)}, u32[]{:S(2)}) collective-permute-start(bf16[128,8,128]{2,1,0:T(8,128)(2,1)S(1)} %fusion.1), channel_id=1, source_target_pairs={{0,1},{1,0},{2,3},{3,2},{4,5},{5,4},{6,7},{7,6},{8,9},{9,8},{10,11... | collective-permute-start | bytes 786440 | tf_op jit(solution)/shard_map/ppermute | solution.py:281
  52.9 6.5 %collective-permute-start.7 = (bf16[128,8,128]{2,1,0:T(8,128)(2,1)S(1)}, bf16[128,8,128]{2,1,0:T(8,128)(2,1)S(1)}, u32[]{:S(2)}, u32[]{:S(2)}) collective-permute-start(bf16[128,8,128]{2,1,0:T(8,128)(2,1)S(1)} %broadcast_select_fusion.refs_0_), channel_id=1, source_target_pairs={{0,8},{1,9},{2,10},{3,11},{4,12},{5,13},{6,14},{7,15},{8,16},{9,17... | collective-permute-start | bytes 786440 | tf_op jit(solution)/shard_map/ppermute | solution.py:278
  53.6 8.3 %collective-permute-start.9 = (bf16[128,8,128]{2,1,0:T(8,128)(2,1)S(1)}, bf16[128,8,128]{2,1,0:T(8,128)(2,1)S(1)}, u32[]{:S(2)}, u32[]{:S(2)}) collective-permute-start(bf16[128,8,128]{2,1,0:T(8,128)(2,1)S(1)} %broadcast_select_fusion.refs_0_), channel_id=1, source_target_pairs={{0,24},{1,25},{2,26},{3,27},{4,28},{5,29},{6,30},{7,31},{8,0},{9,1... | collective-permute-start | bytes 786440 | tf_op jit(solution)/shard_map/ppermute | solution.py:278
  55.7 6.7 %collective-permute-start.8 = (bf16[128,8,128]{2,1,0:T(8,128)(2,1)S(1)}, bf16[128,8,128]{2,1,0:T(8,128)(2,1)S(1)}, u32[]{:S(2)}, u32[]{:S(2)}) collective-permute-start(bf16[128,8,128]{2,1,0:T(8,128)(2,1)S(1)} %broadcast_select_fusion.refs_0_), channel_id=1, source_target_pairs={{0,16},{1,17},{2,18},{3,19},{4,20},{5,21},{6,22},{7,23},{8,24},{9,... | collective-permute-start | bytes 786440 | tf_op jit(solution)/shard_map/ppermute | solution.py:278
  59.5 14.0 %collective-permute-start.13 = (bf16[2,128,8,128]{3,2,1,0:T(8,128)(2,1)S(1)}, bf16[2,128,8,128]{3,2,1,0:T(8,128)(2,1)S(1)}, u32[]{:S(2)}, u32[]{:S(2)}) collective-permute-start(bf16[2,128,8,128]{3,2,1,0:T(8,128)(2,1)S(1)} %pad_maximum_fusion.2), channel_id=1, source_target_pairs={{0,6},{1,7},{2,0},{3,1},{4,2},{5,3},{6,4},{7,5},{8,14},{9,15},{10,... | collective-permute-start | bytes 1572872 | tf_op jit(solution)/shard_map/ppermute | solution.py:278
  60.4 13.1 %collective-permute-start.12 = (bf16[2,128,8,128]{3,2,1,0:T(8,128)(2,1)S(1)}, bf16[2,128,8,128]{3,2,1,0:T(8,128)(2,1)S(1)}, u32[]{:S(2)}, u32[]{:S(2)}) collective-permute-start(bf16[2,128,8,128]{3,2,1,0:T(8,128)(2,1)S(1)} %pad_maximum_fusion.2), channel_id=1, source_target_pairs={{0,2},{1,3},{2,4},{3,5},{4,6},{5,7},{6,0},{7,1},{8,10},{9,11},{10,... | collective-permute-start | bytes 1572872 | tf_op jit(solution)/shard_map/ppermute | solution.py:278
  62.5 22.9 %collective-permute-start.11 = (bf16[2,128,8,128]{3,2,1,0:T(8,128)(2,1)S(1)}, bf16[2,128,8,128]{3,2,1,0:T(8,128)(2,1)S(1)}, u32[]{:S(2)}, u32[]{:S(2)}) collective-permute-start(bf16[2,128,8,128]{3,2,1,0:T(8,128)(2,1)S(1)} %pad_maximum_fusion.1), channel_id=1, source_target_pairs={{0,6},{1,7},{2,0},{3,1},{4,2},{5,3},{6,4},{7,5},{8,14},{9,15},{10,... | collective-permute-start | bytes 1572872 | tf_op jit(solution)/shard_map/ppermute | solution.py:278
  63.2 22.2 %collective-permute-start.10 = (bf16[2,128,8,128]{3,2,1,0:T(8,128)(2,1)S(1)}, bf16[2,128,8,128]{3,2,1,0:T(8,128)(2,1)S(1)}, u32[]{:S(2)}, u32[]{:S(2)}) collective-permute-start(bf16[2,128,8,128]{3,2,1,0:T(8,128)(2,1)S(1)} %pad_maximum_fusion.1), channel_id=1, source_target_pairs={{0,2},{1,3},{2,4},{3,5},{4,6},{5,7},{6,0},{7,1},{8,10},{9,11},{10,... | collective-permute-start | bytes 1572872 | tf_op jit(solution)/shard_map/ppermute | solution.py:278
  85.4 15.5 %collective-permute-start.14 = (bf16[4,128,8,128]{3,2,1,0:T(8,128)(2,1)S(1)}, bf16[4,128,8,128]{3,2,1,0:T(8,128)(2,1)S(1)}, u32[]{:S(2)}, u32[]{:S(2)}) collective-permute-start(bf16[4,128,8,128]{3,2,1,0:T(8,128)(2,1)S(1)} %pad_maximum_fusion), channel_id=1, source_target_pairs={{0,4},{1,5},{2,6},{3,7},{4,0},{5,1},{6,2},{7,3},{8,12},{9,13},{10,... | collective-permute-start | bytes 3145736 | tf_op jit(solution)/shard_map/ppermute | solution.py:278
  87.4 28.4 %collective-permute-start.15 = (bf16[128,768]{1,0:T(8,128)(2,1)S(1)}, bf16[128,768]{1,0:T(8,128)(2,1)S(1)}, u32[]{:S(2)}, u32[]{:S(2)}) collective-permute-start(bf16[128,768]{1,0:T(8,128)(2,1)S(1)} %get-tuple-element.86), channel_id=1, source_target_pairs={{0,64},{64,0},{32,96},{96,32},{1,65},{65,1},{33,97},{97,33},{2,66}... | collective-permute-start | bytes 589832 | tf_op jit(solution)/shard_map/ppermute | solution.py:366
  100.0 15.8 %collective-permute-start.16 = (bf16[256,768]{1,0:T(8,128)(2,1)S(1)}, bf16[256,768]{1,0:T(8,128)(2,1)S(1)}, u32[]{:S(2)}, u32[]{:S(2)}) collective-permute-start(bf16[256,768]{1,0:T(8,128)(2,1)S(1)} %get-tuple-element.87), channel_id=1, source_target_pairs={{0,64},{64,0},{32,96},{96,32},{1,65},{65,1},{33,97},{97,33},{2,66}... | collective-permute-start | bytes 1179656 | tf_op jit(solution)/shard_map/ppermute | solution.py:366
  108.0 7.8 %collective-permute-start.17 = (bf16[128,768]{1,0:T(8,128)(2,1)S(1)}, bf16[128,768]{1,0:T(8,128)(2,1)S(1)}, u32[]{:S(2)}, u32[]{:S(2)}) collective-permute-start(bf16[128,768]{1,0:T(8,128)(2,1)S(1)} %shard_map.54), channel_id=1, source_target_pairs={{0,64},{64,0},{32,96},{96,32},{1,65},{65,1},{33,97},{97,33},{2,66}... | collective-permute-start | bytes 589832 | tf_op jit(solution)/shard_map/ppermute | solution.py:366
  116.5 9.5 %collective-permute-start.18 = (bf16[4,64,768]{2,1,0:T(8,128)(2,1)S(1)}, bf16[4,64,768]{2,1,0:T(8,128)(2,1)S(1)}, u32[]{:S(2)}, u32[]{:S(2)}) collective-permute-start(bf16[4,64,768]{2,1,0:T(8,128)(2,1)S(1)} %get-tuple-element.90), channel_id=1, source_target_pairs={{0,32},{32,0},{64,96},{96,64},{1,33},{33,1},{65,97},{97,65},{2,34}... | collective-permute-start | bytes 1179656 | tf_op jit(solution)/shard_map/ppermute | solution.py:368
